TPU v7x, 128 devices: a whole 4x4x4 slice. The times are simulated.
128 devices in a mesh: row: 8 (over z, core), col: 16 (over y, x).
Axes of the slice: x: 4, y: 4, z: 4, core: 2. Of those that a mesh axis runs over, the one named last changes fastest.
Arguments:
- signal_frames: bfloat16 [65536, 768], P(('row', 'col')), may hold values from -6 to 6
- triple_projection_factors: bfloat16 [768, 2304], replicated, may hold values from -0.21875 to 0.21875
- mixing_projection_factors: bfloat16 [768, 768], replicated, may hold values from -0.21875 to 0.21875
- logit_scaling: float32 [12], replicated, may hold values from 2 to 16
- dispatcher_columns: bfloat16 [768, 256], replicated, may hold values from -0.21875 to 0.21875
- specialist_pick: int32 [65536, 1], P(('row', 'col')), may hold values from 0 to 255; in each aligned block of 512 rows (0 to 511, 512 to 1023, ...) at most 3 rows name the same one
- specialist_entry_factors: bfloat16 [256, 768, 3072], P(('row', 'col')), may hold values from -0.21875 to 0.21875
- specialist_exit_factors: bfloat16 [256, 3072, 768], P(('row', 'col')), may hold values from -0.109375 to 0.109375
Outputs:
- encoded: bfloat16 [65536, 768], P(('row', 'col'))
Inputs may be any that keep to these rules, and one draw needn't show every extreme that they name: `specialist_pick`: within each aligned block of 512 rows no expert is chosen more than 3 times, a bound that some block reaches; every expert is chosen by some row.
All inputs are finite; a program needn't handle non-finite values.
Results may differ from a plain program's by a relative error of at most 0.0056.
Values may be sent and summed in bfloat16 or wider, within the bound.
No kernel may reach another device: no remote copies, remote signals or barrier semaphores. Data moves between devices by JAX's collectives and lax.ppermute only.
A program may use at most 128 MiB of HBM per device.

v0:
```python
import jax
import jax.numpy as jnp
from jax import lax
from jax.sharding import PartitionSpec as P

D = 768
PROBE_TOTAL = 12
LOOKBACK_SPAN = 256


def from_behind(value, axis, steps):
    count = lax.axis_size(axis)
    leading, last = (max(0, -steps), min(count, count - steps))
    return lax.ppermute(value, axis, [(source, source + steps) for source in range(leading, last)])


def layer_norm(matrix):
    matrix = matrix.astype(jnp.float32)
    center = matrix - jnp.mean(matrix, axis=-1, keepdims=True)
    spread = jnp.mean(center * center, axis=-1, keepdims=True)
    return (center * lax.rsqrt(spread + 1e-05)).astype(jnp.bfloat16)


def head_norm(matrix):
    count = matrix.shape[0]
    split = matrix.reshape(count, PROBE_TOTAL, D // PROBE_TOTAL)
    scaled = split * lax.rsqrt(jnp.mean(split * split, axis=-1, keepdims=True) + 1e-06)
    return scaled.reshape(count, D).astype(jnp.bfloat16)


def shards(
    signal_frames,
    triple_projection_factors,
    mixing_projection_factors,
    logit_scaling,
    dispatcher_columns,
    specialist_pick,
    specialist_entry_factors,
    specialist_exit_factors,
):
    tok_rows = signal_frames.shape[0]
    probe_dimension = D // PROBE_TOTAL
    row_count = lax.axis_size("row")
    col_count = lax.axis_size("col")
    devices = row_count * col_count
    experts = dispatcher_columns.shape[1]
    exp_local = specialist_entry_factors.shape[0]
    capacity = max(2, (3 * tok_rows + 2 * experts - 1) // (2 * experts))
    normed = layer_norm(signal_frames)
    projected = jnp.dot(normed, triple_projection_factors, preferred_element_type=jnp.float32)
    asker_tile_entries = head_norm(projected[:, :D])
    lookup_tile_entries = head_norm(projected[:, D : 2 * D])
    payload_tile_entries = projected[:, 2 * D :].astype(jnp.bfloat16)
    stacked = jnp.stack(
        [
            lookup_tile_entries[tok_rows - LOOKBACK_SPAN :],
            payload_tile_entries[tok_rows - LOOKBACK_SPAN :],
        ]
    )
    earlier_pair = from_behind(stacked, ("row", "col"), 1)
    prev_keys = earlier_pair[0]
    prev_values = earlier_pair[1]
    all_keys = jnp.concatenate([prev_keys, lookup_tile_entries], axis=0).reshape(
        LOOKBACK_SPAN + tok_rows, PROBE_TOTAL, probe_dimension
    )
    all_values = jnp.concatenate([prev_values, payload_tile_entries], axis=0).reshape(
        LOOKBACK_SPAN + tok_rows, PROBE_TOTAL, probe_dimension
    )
    raw_similarity_logits = jnp.einsum(
        "qhd,khd->hqk",
        asker_tile_entries.reshape(tok_rows, PROBE_TOTAL, probe_dimension),
        all_keys,
        preferred_element_type=jnp.float32,
    )
    similarity_logits = logit_scaling[:, None, None] * raw_similarity_logits / probe_dimension
    position = lax.axis_index(("row", "col")) * tok_rows
    query_pos = position + jnp.arange(tok_rows, dtype=jnp.int32)
    key_pos = position - LOOKBACK_SPAN + jnp.arange(LOOKBACK_SPAN + tok_rows, dtype=jnp.int32)
    permitted_pairs = (
        (key_pos[None, :] <= query_pos[:, None])
        & (key_pos[None, :] >= query_pos[:, None] - LOOKBACK_SPAN)
        & (key_pos[None, :] >= 0)
    )
    specialist_results = jnp.where(
        permitted_pairs[None], jnp.exp(similarity_logits - logit_scaling[:, None, None]), 0.0
    )
    weights = (specialist_results / jnp.sum(specialist_results, axis=-1, keepdims=True)).astype(
        jnp.bfloat16
    )
    context = jnp.einsum("hqk,khd->qhd", weights, all_values, preferred_element_type=jnp.float32)
    context = context.reshape(tok_rows, D).astype(jnp.bfloat16)
    hidden = (
        signal_frames.astype(jnp.float32)
        + jnp.dot(context, mixing_projection_factors, preferred_element_type=jnp.float32)
    ).astype(jnp.bfloat16)
    routed = layer_norm(hidden)
    logits = jnp.dot(routed, dispatcher_columns, preferred_element_type=jnp.float32)
    chosen = specialist_pick[:, 0]
    onehot = chosen[:, None] == jnp.arange(experts, dtype=jnp.int32)[None, :]
    gate_value = jax.nn.sigmoid(jnp.sum(jnp.where(onehot, logits, 0.0), axis=1))
    same_expert = chosen[:, None] == chosen[None, :]
    earlier = (
        jnp.arange(tok_rows, dtype=jnp.int32)[:, None]
        > jnp.arange(tok_rows, dtype=jnp.int32)[None, :]
    )
    slot_index = jnp.sum((same_expert & earlier).astype(jnp.int32), axis=1)
    flat_index = chosen * capacity + slot_index
    buffer = jnp.zeros((experts * capacity, D), jnp.bfloat16).at[flat_index].set(routed)
    arrived = lax.all_to_all(
        buffer.reshape(devices, exp_local, capacity, D),
        ("row", "col"),
        split_axis=0,
        concat_axis=0,
        tiled=True,
    )
    expert_hidden = jax.nn.relu(
        jnp.einsum(
            "necd,edf->necf", arrived, specialist_entry_factors, preferred_element_type=jnp.float32
        )
    ).astype(jnp.bfloat16)
    expert_out = jnp.einsum(
        "necf,efd->necd", expert_hidden, specialist_exit_factors, preferred_element_type=jnp.float32
    ).astype(jnp.bfloat16)
    returned = lax.all_to_all(expert_out, ("row", "col"), split_axis=0, concat_axis=0, tiled=True)
    returned = returned.reshape(experts * capacity, D)
    picked = returned[flat_index]
    return (hidden.astype(jnp.float32) + gate_value[:, None] * picked.astype(jnp.float32)).astype(
        jnp.bfloat16
    )


def solution(mesh):
    in_specs = (
        P(("row", "col"), None),
        P(),
        P(),
        P(),
        P(),
        P(("row", "col"), None),
        P(("row", "col"), None, None),
        P(("row", "col"), None, None),
    )
    out_specs = P(("row", "col"), None)
    return jax.shard_map(shards, mesh=mesh, in_specs=in_specs, out_specs=out_specs, check_vma=False)
```

profile of v0, /device:TPU:1, one launch (start us, length us, event | category | flops | bytes accessed | tf_op | source)
XLA Modules:
  0.0 150.7 jit_solution(2624765218168627835)
XLA Ops:
  0.0 1.5 convert_reduce_fusion.1
  1.5 1.6 %fusion.15 = f32[512]{0:T(512)S(1)} fusion(bf16[512,768]{1,0:T(8,128)(2,1)} %param.8, f32[512]{0:T(512)S(1)} %broadcast_multiply_fusion.1), kind=kLoop, calls=%fused_computation.24 | loop fusion | flops 1572352 | bytes 790528 | tf_op jit(solution)/shard_map/reduce_sum | solution.py:20
  3.1 3.5 %fusion.53 = (bf16[512,2304]{1,0:T(8,128)(2,1)}, f32[512,2304]{1,0:T(8,128)S(1)}) fusion(bf16[768,2304]{1,0:T(8,128)(2,1)S(1)} %copy-done, bf16[512,768]{1,0:T(8,128)(2,1)S(1)} %copy-done.5, f32[512]{0:T(512)S(1)} %add_rsqrt_fusion.3, f32[512]{0:T(512)S(1)} %broadcast_multiply_fusion.1), kind=kOutput, calls=%fused_computation.76 | convolution fusion | flops 1814691840 | bytes 11407360 | tf_op jit(solution)/shard_map/dot_general | solution.py:50
  6.6 1.5 %slice_multiply_fusion.1 = (f32[512,768]{1,0:T(8,128)}, f32[512,768]{1,0:T(8,128)S(1)}) fusion(f32[512,2304]{1,0:T(8,128)S(1)} %get-tuple-element.12), kind=kLoop, calls=%fused_computation.33 | loop fusion | flops 786432 | bytes 6291456 | tf_op jit(solution)/shard_map/mul | solution.py:27
  8.1 1.1 copy-done.2
  9.2 1.9 %copy.49 = f32[512,768]{0,1:T(8,128)S(1)} copy(f32[512,768]{1,0:T(8,128)} %get-tuple-element.7) | data formatting | bytes 3145728 | tf_op jit(solution)/shard_map/mul | solution.py:27
  11.1 0.2 reduce_sum.85
  11.3 0.2 mul.90
  11.5 1.7 %copy.50 = f32[512,768]{1,0:T(8,128)} copy(f32[512,768]{0,1:T(8,128)S(1)} %bitcast.52) | data formatting | bytes 3145728 | tf_op jit(solution)/shard_map/mul | solution.py:27
  13.2 0.5 copy.53
  13.7 0.2 reduce_sum.86
  13.9 0.2 mul.98
  14.1 1.7 %copy.54 = f32[512,768]{1,0:T(8,128)} copy(f32[512,768]{0,1:T(8,128)S(1)} %bitcast.53) | data formatting | bytes 3145728 | tf_op jit(solution)/shard_map/mul | solution.py:27
  15.8 3.7 %multiply_convert_fusion.1 = (bf16[512,768]{1,0:T(8,128)(2,1)S(1)}, bf16[512,768]{1,0:T(8,128)(2,1)}) fusion(f32[512,768]{1,0:T(8,128)S(1)} %copy-done.4, f32[512,2304]{1,0:T(8,128)} %copy-done.2, f32[512,768]{1,0:T(8,128)} %copy.54), kind=kLoop, calls=%fused_computation.29 | loop fusion | flops 1572864 | bytes 7864320 | tf_op jit(solution)/shard_map/convert_element_type | solution.py:28
  19.5 0.1 slice_bitcast_fusion
  19.6 1.0 pad_maximum_fusion
  20.5 4.1 %collective-permute-start = (bf16[2,256,768]{2,1,0:T(8,128)(2,1)}, bf16[2,256,768]{2,1,0:T(8,128)(2,1)}, u32[]{:S(2)}, u32[]{:S(2)}) collective-permute-start(bf16[2,256,768]{2,1,0:T(8,128)(2,1)} %pad_maximum_fusion), channel_id=1, source_target_pairs={{0,1},{1,2},{2,3},{3,4},{4,5},{5,6},{6,7},{7,8},{8,9},{9,10},{10,1... | collective-permute-start | bytes 2359304 | tf_op jit(solution)/shard_map/ppermute | solution.py:14
  24.6 0.1 slice.36
  24.7 0.0 copy-start.7
  24.7 0.3 copy.57
  25.0 0.0 copy-start.10
  25.0 1.2 copy.52
  26.2 0.3 copy.55
  26.6 0.2 convert_reduce_fusion.2
  26.8 0.4 and_and_fusion
  27.3 19.0 %collective-permute-done = bf16[2,256,768]{2,1,0:T(8,128)(2,1)} collective-permute-done((bf16[2,256,768]{2,1,0:T(8,128)(2,1)}, bf16[2,256,768]{2,1,0:T(8,128)(2,1)}, u32[]{:S(2)}, u32[]{:S(2)}) %collective-permute-start) | collective-permute-done | bytes 786464 | tf_op jit(solution)/shard_map/ppermute | solution.py:14
  46.3 1.2 fusion.52
  47.4 0.2 copy.51
  47.6 0.2 copy.56
  47.8 10.0 %fusion = (f32[12,512]{1,0:T(8,128)S(1)}, f32[12,512,768]{2,1,0:T(8,128)}) fusion(f32[12]{0:T(128)S(1)} %copy-done.15, pred[512,768]{1,0:T(8,128)(4,1)S(1)} %and_and_fusion, bf16[512,12,64]{0,2,1:T(8,128)(2,1)S(1)} %bitcast.56, bf16[512,12,64]{0,2,1:T(8,128)(2,1)S(1)} %bitcast.54, bf16[256,12,64]{0,2,1:T(8,128)(2,1)S(1)} %bitcast.58), kind=kOutput, calls=%fused_computation.4 | convolution fusion | flops 629925888 | bytes 21258288 | tf_op jit(solution)/shard_map/qhd,khd->hqk/dot_general | solution.py:69
  57.8 10.2 %fusion.29 = bf16[12,64,512]{2,1,0:T(8,128)(2,1)S(1)} fusion(f32[12,512,768]{2,1,0:T(8,128)} %get-tuple-element.14, f32[12,512]{1,0:T(8,128)S(1)} %get-tuple-element.13, f32[12]{0:T(128)S(1)} %copy-done.15, pred[512,768]{1,0:T(8,128)(4,1)S(1)} %and_and_fusion, bf16[512,12,64]{0,2,1:T(8,128)(2,1)S(1)} %bitcast.55, bf16[256,12,64]{0,2,1:T(8,128)(2,1)S(1)} %bitcast.57), kind=kOutput, calls=%fused_computation.35 | convolution fusion | flops 635043840 | bytes 21258288 | tf_op jit(solution)/shard_map/hqk,khd->qhd/dot_general | solution.py:90
  68.0 0.9 convert_reduce_fusion
  69.0 0.4 fusion.13
  69.3 3.2 %scatter_custom_fusion = bf16[768,768]{1,0:T(8,128)(2,1)S(1)} fusion(s32[512]{0:T(512)S(1)} %bitcast.61, bf16[]{:T(256)} %constant.47.clone.1, bf16[512,768]{1,0:T(8,128)(2,1)S(1)} %get-tuple-element.16, f32[512]{0:T(512)S(1)} %add_rsqrt_fusion.2, f32[512]{0:T(512)S(1)} %broadcast_multiply_fusion), kind=kCustom, calls=%fused_computation.53 | custom fusion | flops 1572864 | bytes 1970178 | tf_op jit(solution)/shard_map/scatter | solution.py:108
  72.5 0.6 reshape.164
  73.2 1.0 copy.58
  74.2 0.0 slice-start
  74.2 27.3 %all_to_all.10 = bf16[128,2,3,768]{3,1,2,0:T(2,128)(2,1)S(1)} all-to-all(bf16[128,2,3,768]{3,1,2,0:T(2,128)(2,1)S(1)} %copy.58), channel_id=1, replica_groups=mesh['row'=8,'col'=16] {'row','col'}, dimensions={0} | all-to-all | bytes 2359296 | tf_op jit(solution)/shard_map/all_to_all | solution.py:109
  101.5 7.9 %maximum_convert_fusion = bf16[2,128,3,3072]{3,1,2,0:T(8,128)(2,1)S(1)} fusion(bf16[2,768,3072]{2,1,0:T(8,128)(2,1)} %param.14, bf16[128,2,3,768]{3,1,2,0:T(2,128)(2,1)S(1)} %all_to_all.10), kind=kOutput, calls=%fused_computation.9 | convolution fusion | flops 3628597248 | bytes 15335424 | tf_op jit(solution)/shard_map/necd,edf->necf/dot_general | solution.py:117
  109.4 3.8 %fusion.24 = bf16[128,2,3,768]{3,0,2,1:T(8,128)(2,1)S(1)} fusion(bf16[2,3072,768]{2,1,0:T(8,128)(2,1)S(1)} %bitcast.65, bf16[2,128,3,3072]{3,1,2,0:T(8,128)(2,1)S(1)} %maximum_convert_fusion), kind=kOutput, calls=%fused_computation.34 | convolution fusion | flops 3624468480 | bytes 15335424 | tf_op jit(solution)/shard_map/necf,efd->necd/dot_general | solution.py:121
  113.2 2.2 %copy.60 = bf16[128,2,3,768]{3,1,2,0:T(2,128)(2,1)} copy(bf16[128,2,3,768]{3,0,2,1:T(8,128)(2,1)S(1)} %fusion.24) | data formatting | bytes 2359296 | tf_op jit(solution)/shard_map/convert_element_type | solution.py:123
  115.5 4.8 %all-to-all-start.1 = ((bf16[128,2,3,768]{3,1,2,0:T(2,128)(2,1)}), bf16[128,2,3,768]{3,1,2,0:T(2,128)(2,1)S(1)}, u32[]{:S(2)}, u32[]{:S(2)}) async-start(bf16[128,2,3,768]{3,1,2,0:T(2,128)(2,1)} %copy.60), calls=%async_computation.1 | async-start | bytes 2359296 | tf_op jit(solution)/shard_map/all_to_all | solution.py:124
  120.3 0.6 fusion.38
  121.0 19.7 %all-to-all-done.1 = bf16[128,2,3,768]{3,1,2,0:T(2,128)(2,1)S(1)} async-done(((bf16[128,2,3,768]{3,1,2,0:T(2,128)(2,1)}), bf16[128,2,3,768]{3,1,2,0:T(2,128)(2,1)S(1)}, u32[]{:S(2)}, u32[]{:S(2)}) %all-to-all-start.1) | async-done | bytes 1179680 | tf_op jit(solution)/shard_map/all_to_all | solution.py:124
  140.6 0.6 copy.61
  141.3 2.2 %reshape.165 = bf16[768,768]{1,0:T(8,128)(2,1)} reshape(bf16[128,2,3,768]{3,2,1,0:T(4,128)(2,1)S(1)} %copy.61) | data formatting | bytes 2359296 | tf_op jit(solution)/shard_map/reshape | solution.py:125
  143.5 4.7 %gather_fusion = bf16[512,768]{1,0:T(8,128)(2,1)} fusion(bf16[768,768]{1,0:T(8,128)(2,1)} %reshape.165, s32[1024]{0:T(1024)S(1)} %pad_clamp_fusion), kind=kCustom, calls=%fused_computation | custom fusion | bytes 1574912 | tf_op jit(solution)/shard_map/gather | solution.py:126
  148.1 2.5 %fusion.18 = bf16[512,768]{1,0:T(8,128)(2,1)} fusion(bf16[512,768]{1,0:T(8,128)(2,1)} %copy-done.3, bf16[512,768]{1,0:T(8,128)(2,1)} %gather_fusion, f32[512]{0:T(512)S(1)} %add_divide_fusion), kind=kLoop, calls=%fused_computation.27 | loop fusion | flops 1966080 | bytes 2361344 | tf_op jit(solution)/shard_map/convert_element_type | solution.py:127
  (47 shorter events, 0.2 us)
Async XLA Ops:
  0.0 3.0 %copy-start = (bf16[768,2304]{1,0:T(8,128)(2,1)S(1)}, bf16[768,2304]{1,0:T(8,128)(2,1)}, u32[]{:S(2)}) copy-start(bf16[768,2304]{1,0:T(8,128)(2,1)} %param.9) | copy-start | bytes 10616836
  0.0 3.0 %copy-start.5 = (bf16[512,768]{1,0:T(8,128)(2,1)S(1)}, bf16[512,768]{1,0:T(8,128)(2,1)}, u32[]{:S(2)}) copy-start(bf16[512,768]{1,0:T(8,128)(2,1)} %param.8) | copy-start | bytes 2359300
  6.6 2.6 %copy-start.2 = (f32[512,2304]{1,0:T(8,128)}, f32[512,2304]{1,0:T(8,128)S(1)}, u32[]{:S(2)}) copy-start(f32[512,2304]{1,0:T(8,128)S(1)} %get-tuple-element.12) | copy-start | bytes 14155780
  14.1 1.7 %copy-start.4 = (f32[512,768]{1,0:T(8,128)S(1)}, f32[512,768]{1,0:T(8,128)}, u32[]{:S(2)}) copy-start(f32[512,768]{1,0:T(8,128)} %copy.50) | copy-start | bytes 4718596
  15.8 3.7 %copy-start.9 = (bf16[512,2304]{1,0:T(8,128)(2,1)S(1)}, bf16[512,2304]{1,0:T(8,128)(2,1)}, u32[]{:S(2)}) copy-start(bf16[512,2304]{1,0:T(8,128)(2,1)} %get-tuple-element.11) | copy-start | bytes 7077892
  20.5 25.7 %collective-permute-start = (bf16[2,256,768]{2,1,0:T(8,128)(2,1)}, bf16[2,256,768]{2,1,0:T(8,128)(2,1)}, u32[]{:S(2)}, u32[]{:S(2)}) collective-permute-start(bf16[2,256,768]{2,1,0:T(8,128)(2,1)} %pad_maximum_fusion), channel_id=1, source_target_pairs={{0,1},{1,2},{2,3},{3,4},{4,5},{5,6},{6,7},{7,8},{8,9},{9,10},{10,1... | collective-permute-start | bytes 2359304 | tf_op jit(solution)/shard_map/ppermute | solution.py:14
  24.7 1.5 %copy-start.7 = (bf16[512,768]{1,0:T(8,128)(2,1)S(1)}, bf16[512,768]{1,0:T(8,128)(2,1)}, u32[]{:S(2)}) copy-start(bf16[512,768]{1,0:T(8,128)(2,1)} %get-tuple-element.6) | copy-start | bytes 2359300
  25.0 1.5 %copy-start.10 = (s32[512,1]{0,1:T(1,128)S(1)}, s32[512,1]{0,1:T(1,128)}, u32[]{:S(2)}) copy-start(s32[512,1]{0,1:T(1,128)} %param.13) | copy-start | bytes 6148
  27.3 20.5 %copy-start.15 = (f32[12]{0:T(128)S(1)}, f32[12]{0:T(128)}, u32[]{:S(2)}) copy-start(f32[12]{0:T(128)} %param.11) | copy-start | bytes 148
  47.8 10.1 %copy-start.8 = (bf16[512,768]{0,1:T(8,128)(2,1)S(1)}, bf16[512,768]{0,1:T(8,128)(2,1)}, u32[]{:S(2)}) copy-start(bf16[512,768]{0,1:T(8,128)(2,1)} %copy.52) | copy-start | bytes 2359300
  57.8 10.2 %copy-start.6 = (bf16[512,768]{1,0:T(8,128)(2,1)S(1)}, bf16[512,768]{1,0:T(8,128)(2,1)}, u32[]{:S(2)}) copy-start(bf16[512,768]{1,0:T(8,128)(2,1)} %param.8) | copy-start | bytes 2359300
  57.8 10.2 %copy-start.13 = (bf16[768,768]{1,0:T(8,128)(2,1)S(1)}, bf16[768,768]{1,0:T(8,128)(2,1)}, u32[]{:S(2)}) copy-start(bf16[768,768]{1,0:T(8,128)(2,1)} %param.10) | copy-start | bytes 3538948
  68.9 51.4 %copy-start.3 = (bf16[512,768]{1,0:T(8,128)(2,1)}, bf16[512,768]{1,0:T(8,128)(2,1)S(1)}, u32[]{:S(2)}) copy-start(bf16[512,768]{1,0:T(8,128)(2,1)S(1)} %get-tuple-element.16) | copy-start | bytes 2359300
  69.3 3.9 %copy-start.11 = (f32[512]{0:T(512)}, f32[512]{0:T(512)S(1)}, u32[]{:S(2)}) copy-start(f32[512]{0:T(512)S(1)} %add_rsqrt_fusion.2) | copy-start | bytes 6148
  74.2 35.2 %slice-start = ((s8[9437184]{0:T(1024)(128)(4,1)}), s8[4194304]{0:T(1024)(128)(4,1)S(1)}, s32[]{:S(2)}) async-start(s8[9437184]{0:T(1024)(128)(4,1)} %bitcast.64), calls=%async_computation.2 | async-start | bytes 8388608
  101.5 7.9 %slice-start.1 = ((s8[9437184]{0:T(1024)(128)(4,1)}), s8[4194304]{0:T(1024)(128)(4,1)S(1)}, s32[]{:S(2)}) async-start(s8[9437184]{0:T(1024)(128)(4,1)} %bitcast.64), calls=%async_computation.3 | async-start | bytes 8388608
  101.5 7.9 %slice-start.2 = ((s8[9437184]{0:T(1024)(128)(4,1)}), s8[1048576]{0:T(1024)(128)(4,1)S(1)}, s32[]{:S(2)}) async-start(s8[9437184]{0:T(1024)(128)(4,1)} %bitcast.64), calls=%async_computation.4 | async-start | bytes 2097152
  115.5 4.9 %copy-start.12 = (f32[512]{0:T(512)S(1)}, f32[512]{0:T(512)}, u32[]{:S(2)}) copy-start(f32[512]{0:T(512)} %copy-done.11) | copy-start | bytes 6148
  115.5 4.9 %copy-start.14 = (bf16[768,256]{1,0:T(8,128)(2,1)S(1)}, bf16[768,256]{1,0:T(8,128)(2,1)}, u32[]{:S(2)}) copy-start(bf16[768,256]{1,0:T(8,128)(2,1)} %param.12) | copy-start | bytes 1179652
  115.5 25.2 %all-to-all-start.1 = ((bf16[128,2,3,768]{3,1,2,0:T(2,128)(2,1)}), bf16[128,2,3,768]{3,1,2,0:T(2,128)(2,1)S(1)}, u32[]{:S(2)}, u32[]{:S(2)}) async-start(bf16[128,2,3,768]{3,1,2,0:T(2,128)(2,1)} %copy.60), calls=%async_computation.1 | async-start | bytes 2359296 | tf_op jit(solution)/shard_map/all_to_all | solution.py:124
  143.5 7.2 %copy-start.1 = (bf16[768,2304]{1,0:T(8,128)(2,1)S(1)}, bf16[768,2304]{1,0:T(8,128)(2,1)}, u32[]{:S(2)}) copy-start(bf16[768,2304]{1,0:T(8,128)(2,1)} %param.9) | copy-start | bytes 10616836
where the time goes:
time: 151 us
  waiting for transfers between devices  38.7 us (26%)
  matrix products  36.9 us (24%)
  blocking collectives  27.3 us (18%)
  local copies, waits for them, and re-layouts  22 us (15%)
  other arithmetic  16.5 us (11%)
  starting transfers between devices  8.94 us (6%)
    all_to_all x1, blocking collectives, shards(): lax.all_to_all(buffer.reshape(devices, exp_local, capacity, D), ('row', '...  27.3 us
    all_to_all x1, waiting for transfers between devices, shards(): lax.all_to_all(expert_out, ('row', 'col'), split_axis=0, concat_axis=0, t...  19.7 us
    ppermute x1, waiting for transfers between devices, from_behind(): lax.ppermute(value, axis, [(source, source + steps) for source in range(l...  19 us
    dot_general x1, matrix products, shards(): jnp.einsum('hqk,khd->qhd', weights, all_values, preferred_element_type=jn...  10.2 us
    dot_general x1, matrix products, shards(): jnp.einsum('qhd,khd->hqk', asker_tile_entries.reshape(tok_rows, PROBE_TOT...  10 us
    dot_general x1, matrix products, shards(): jnp.einsum('necd,edf->necf', arrived, specialist_entry_factors, preferred...  7.89 us
    all_to_all x1, starting transfers between devices, shards(): lax.all_to_all(expert_out, ('row', 'col'), split_axis=0, concat_axis=0, t...  4.83 us
    gather x1, local copies, waits for them, and re-layouts, shards(): picked = returned[flat_index]  4.65 us
  transfers between devices with their start and end apart: 2, of which 2 were waited for; matrix products, arithmetic and copies ran while one was open for 2% of the time, Pallas kernels for 0%

commit v1 on v0

v1 whole, which is shorter than its diff:
```python
import math

import jax
import jax.numpy as jnp
from jax import lax
from jax.experimental import pallas as pl
from jax.experimental.pallas import tpu as pltpu
from jax.sharding import PartitionSpec as P

D = 768
HEADS = 12
LOOK = 256
T = 512
FF = 3072
CAP = 3
SLOTS = 768
PAIRS = HEADS // 2
LANES = 128
AXES = ("row", "col")
BF = jnp.bfloat16
F32 = jnp.float32
MB = 1 << 20


def dot(a, b):
    return jnp.dot(a, b, preferred_element_type=F32)


def dot_t(a, b):
    return lax.dot_general(a, b, (((1,), (1,)), ((), ())), preferred_element_type=F32)


def norm_rows(value):
    center = value - jnp.mean(value, axis=-1, keepdims=True)
    spread = jnp.mean(center * center, axis=-1, keepdims=True)
    return (center * lax.rsqrt(spread + 1e-05)).astype(BF)


def head_blocks():
    down = lax.shift_right_logical(lax.broadcasted_iota(jnp.int32, (256, 256), 0), 6)
    across = lax.shift_right_logical(lax.broadcasted_iota(jnp.int32, (256, 256), 1), 6)
    return jnp.where(down == across, 1.0, 0.0).astype(BF)


def head_norm(value, blocks):
    square = (value * value).astype(BF)
    return value * lax.rsqrt(dot(square, blocks) * (1.0 / 64) + 1e-06)


def triangles():
    down = lax.broadcasted_iota(jnp.int32, (128, 128), 0)
    across = lax.broadcasted_iota(jnp.int32, (128, 128), 1)
    behind = jnp.where(across >= down, 1.0, 0.0).astype(BF)
    ahead = jnp.where(across <= down, 1.0, 0.0).astype(BF)
    return behind, ahead


def half_lanes(half):
    lane = lax.broadcasted_iota(jnp.int32, (1, LANES), 1)
    mine = (lane < 64) if half == 0 else (lane >= 64)
    return jnp.where(mine, 1.0, 0.0).astype(BF)


def weigh(part):
    return jnp.exp2(part).astype(BF)


def behind_weights(scores, behind):
    top = jnp.concatenate([weigh(scores[:128, :128]) * behind, weigh(scores[:128, 128:])], axis=1)
    low = jnp.concatenate([jnp.zeros((128, 128), BF), weigh(scores[128:, 128:]) * behind], axis=1)
    return jnp.concatenate([top, low], axis=0)


def own_weights(scores, ahead):
    top = jnp.concatenate([weigh(scores[:128, :128]) * ahead, jnp.zeros((128, 128), BF)], axis=1)
    low = jnp.concatenate([weigh(scores[128:, :128]), weigh(scores[128:, 128:]) * ahead], axis=1)
    return jnp.concatenate([top, low], axis=0)


def payload(values, half, ones):
    mask = half_lanes(half)
    return jnp.concatenate([values * mask, ones * mask], axis=1)


def first_kernel(x_ref, w_ref, mix_ref, scale_ref, q_out, acc_out, hid_out, rou_out, normed, q_s, k_s, v_s, ctx):
    for r in range(0, T, 32):
        normed[r : r + 32, :] = norm_rows(x_ref[r : r + 32, :].astype(F32))
    blocks = head_blocks()
    for g in range(3):
        c = slice(g * 256, g * 256 + 256)
        value = head_norm(dot(normed[...], w_ref[:, g * 256 : g * 256 + 256]), blocks)
        q_s[:, c] = (value * scale_ref[:, c]).astype(BF)
        value = head_norm(dot(normed[...], w_ref[:, D + g * 256 : D + g * 256 + 256]), blocks)
        k_s[:, c] = value.astype(BF)
        v_s[:, c] = dot(normed[...], w_ref[:, 2 * D + g * 256 : 2 * D + g * 256 + 256]).astype(BF)
    q_out[...] = q_s[:LOOK, :]
    behind, ahead = triangles()
    ones = jnp.ones((LOOK, LANES), BF)
    for pair in range(PAIRS):
        c = slice(pair * LANES, pair * LANES + LANES)
        low = jnp.zeros((LOOK, 256), F32)
        high = jnp.zeros((LOOK, 256), F32)
        for half in range(2):
            mask = half_lanes(half)
            q0 = q_s[:LOOK, c] * mask
            q1 = q_s[LOOK:, c] * mask
            k0 = k_s[:LOOK, c]
            k1 = k_s[LOOK:, c]
            v0 = payload(v_s[:LOOK, c], half, ones)
            v1 = payload(v_s[LOOK:, c], half, ones)
            low += dot(own_weights(dot_t(q0, k0), ahead), v0)
            high += dot(behind_weights(dot_t(q1, k0), behind), v0)
            high += dot(own_weights(dot_t(q1, k1), ahead), v1)
        acc_out[:, pair * 256 : pair * 256 + 256] = low
        ctx[:, c] = (high[:, :LANES] / high[:, LANES:]).astype(BF)
    finish(ctx, mix_ref, x_ref, LOOK, hid_out, rou_out, 0)


def finish(ctx, mix_ref, x_ref, x_at, hid_out, rou_out, at):
    for r in range(0, LOOK, 128):
        mixed = dot(ctx[r : r + 128, :], mix_ref[...])
        for s in range(r, r + 128, 32):
            hidden = (x_ref[x_at + s : x_at + s + 32, :].astype(F32) + mixed[s - r : s - r + 32, :]).astype(BF)
            hid_out[at + s : at + s + 32, :] = hidden
            rou_out[at + s : at + s + 32, :] = norm_rows(hidden.astype(F32))


def second_kernel(valid_ref, halo_ref, w_ref, mix_ref, x_ref, q_ref, acc_ref, hid_ref, rou_ref, row_ref, buf_out, hid_out, rou_out, normed, k_s, v_s, ctx):
    for r in range(0, LOOK, 32):
        normed[r : r + 32, :] = norm_rows(halo_ref[r : r + 32, :].astype(F32))
    blocks = head_blocks()
    for g in range(3):
        c = slice(g * 256, g * 256 + 256)
        k_s[:, c] = head_norm(dot(normed[...], w_ref[:, D + g * 256 : D + g * 256 + 256]), blocks).astype(BF)
        v_s[:, c] = dot(normed[...], w_ref[:, 2 * D + g * 256 : 2 * D + g * 256 + 256]).astype(BF)
    behind, _ = triangles()
    ones = jnp.full((LOOK, LANES), valid_ref[0].astype(F32)).astype(BF)
    for pair in range(PAIRS):
        c = slice(pair * LANES, pair * LANES + LANES)
        low = acc_ref[:, pair * 256 : pair * 256 + 256]
        for half in range(2):
            q0 = q_ref[:, c] * half_lanes(half)
            low += dot(behind_weights(dot_t(q0, k_s[:, c]), behind), payload(v_s[:, c] * ones, half, ones))
        ctx[:, c] = (low[:, :LANES] / low[:, LANES:]).astype(BF)
    finish(ctx, mix_ref, x_ref, 0, hid_out, rou_out, 0)
    hid_out[LOOK:, :] = hid_ref[...]
    rou_out[LOOK:, :] = rou_ref[...]
    for s in range(0, SLOTS, 256):
        place = lax.broadcasted_iota(jnp.int32, (256, T), 0) + s
        pick = jnp.where(place == row_ref[...], 1.0, 0.0).astype(BF)
        buf_out[s : s + 256, :] = dot(pick, rou_out[...]).astype(BF)


def expert_kernel(in_ref, first_ref, second_ref, out_ref, rows, total, done):
    expert = pl.program_id(0)
    chunk = pl.program_id(1)

    @pl.when(chunk == 0)
    def _():
        down = lax.broadcasted_iota(jnp.int32, (128, 256), 0)
        across = lax.broadcasted_iota(jnp.int32, (128, 256), 1)
        pick = jnp.where(across == 2 * down + expert, 1.0, 0.0).astype(BF)
        for b in range(3):
            rows[b * 128 : b * 128 + 128, :] = dot(pick, in_ref[b * 256 : b * 256 + 256, :]).astype(BF)

    hidden = jnp.maximum(dot(rows[...], first_ref[0]), 0.0).astype(BF)
    part = dot(hidden, second_ref[0])

    @pl.when(chunk == 0)
    def _():
        total[...] = part

    @pl.when(chunk > 0)
    def _():
        total[...] += part

    @pl.when(chunk == pl.num_programs(1) - 1)
    def _():
        done[expert] = total[...].astype(BF)

    @pl.when((chunk == pl.num_programs(1) - 1) & (expert == 1))
    def _():
        down = lax.broadcasted_iota(jnp.int32, (256, 128), 0)
        across = lax.broadcasted_iota(jnp.int32, (256, 128), 1)
        put0 = jnp.where(down == 2 * across, 1.0, 0.0).astype(BF)
        put1 = jnp.where(down == 2 * across + 1, 1.0, 0.0).astype(BF)
        for b in range(3):
            r = slice(b * 128, b * 128 + 128)
            out_ref[b * 256 : b * 256 + 256, :] = (dot(put0, done[0, r, :]) + dot(put1, done[1, r, :])).astype(BF)


def gate_kernel(rou_ref, columns_ref, pick_ref, gate_out):
    logits = dot(rou_ref[...], columns_ref[...])
    across = lax.broadcasted_iota(jnp.int32, logits.shape, 1)
    chosen = jnp.sum(jnp.where(across == pick_ref[...], logits, 0.0), axis=1, keepdims=True)
    gate_out[...] = 1.0 / (1.0 + jnp.exp(-chosen))


def last_kernel(back_ref, hid_ref, gate_ref, col_ref, out_ref):
    for r in range(0, T, 256):
        across = lax.broadcasted_iota(jnp.int32, (256, SLOTS), 1)
        pick = jnp.where(across == col_ref[r : r + 256, :], 1.0, 0.0).astype(BF)
        picked = dot(pick, back_ref[...])
        gate = gate_ref[r : r + 256, :]
        out_ref[r : r + 256, :] = (hid_ref[r : r + 256, :].astype(F32) + gate * picked).astype(BF)


def params(limit):
    return pltpu.CompilerParams(vmem_limit_bytes=limit * MB)


def shape(*dims, dtype=BF):
    return jax.ShapeDtypeStruct(dims, dtype)


def cost(flops, moved, exps=0):
    return pl.CostEstimate(flops=flops, bytes_accessed=moved, transcendentals=exps)


def shards(x, triple, mixing, scaling, columns, pick, entry, exits):
    steps = [(i, i + 1) for i in range(127)]
    halo = lax.ppermute(x[T - LOOK :], AXES, steps)
    scale = jnp.repeat(scaling * (math.log2(math.e) / 64), 64)[None, :]
    chosen = pick[:, 0]
    order = jnp.arange(T, dtype=jnp.int32)
    same = chosen[:, None] == chosen[None, :]
    slot_row = jnp.sum((same & (order[:, None] < order[None, :])).astype(jnp.int32), axis=0)
    slot_col = jnp.sum((same & (order[None, :] < order[:, None])).astype(jnp.int32), axis=1)
    place = (chosen >> 1) * (2 * CAP) + (chosen & 1)
    flat_row = (place + 2 * slot_row)[None, :]
    flat_col = (place + 2 * slot_col)[:, None]
    q0, acc0, hid1, rou1 = pl.pallas_call(
        first_kernel,
        out_shape=(shape(LOOK, D), shape(LOOK, 2 * D, dtype=F32), shape(LOOK, D), shape(LOOK, D)),
        scratch_shapes=[pltpu.VMEM((T, D), BF)] * 4 + [pltpu.VMEM((LOOK, D), BF)],
        compiler_params=params(40),
        cost_estimate=cost(4 * 10**9, 8 * MB),
        name="first",
    )(x, triple, mixing, scale)
    valid = jnp.minimum(lax.axis_index(AXES), 1).astype(jnp.int32).reshape(1)
    vmem = pl.BlockSpec(memory_space=pltpu.VMEM)
    buf, hidden, routed = pl.pallas_call(
        second_kernel,
        out_shape=(shape(SLOTS, D), shape(T, D), shape(T, D)),
        in_specs=[pl.BlockSpec(memory_space=pltpu.SMEM)] + [vmem] * 9,
        scratch_shapes=[pltpu.VMEM((LOOK, D), BF)] * 4,
        compiler_params=params(40),
        cost_estimate=cost(2 * 10**9, 8 * MB),
        name="second",
    )(valid, halo, triple, mixing, x, q0, acc0, hid1, rou1, flat_row)
    arrived = lax.all_to_all(buf.reshape(128, CAP, 2, D), AXES, split_axis=0, concat_axis=0, tiled=True)
    chunks = 4
    width = FF // chunks
    out = pl.pallas_call(
        expert_kernel,
        out_shape=shape(SLOTS, D),
        grid=(2, chunks),
        in_specs=[
            pl.BlockSpec((SLOTS, D), lambda e, f: (0, 0)),
            pl.BlockSpec((1, D, width), lambda e, f: (e, 0, f)),
            pl.BlockSpec((1, width, D), lambda e, f: (e, f, 0)),
        ],
        out_specs=pl.BlockSpec((SLOTS, D), lambda e, f: (0, 0)),
        scratch_shapes=[pltpu.VMEM((SLOTS // 2, D), BF), pltpu.VMEM((SLOTS // 2, D), F32), pltpu.VMEM((2, SLOTS // 2, D), BF)],
        compiler_params=params(32),
        cost_estimate=cost(7 * 10**9, 20 * MB),
        name="experts",
    )(arrived.reshape(SLOTS, D), entry, exits)
    back = lax.all_to_all(out.reshape(128, CAP, 2, D), AXES, split_axis=0, concat_axis=0, tiled=True)
    gate = pl.pallas_call(
        gate_kernel,
        out_shape=shape(T, 1, dtype=F32),
        compiler_params=params(16),
        cost_estimate=cost(2 * 10**8, 2 * MB),
        name="gate",
    )(routed, columns, pick)
    return pl.pallas_call(
        last_kernel,
        out_shape=shape(T, D),
        compiler_params=params(24),
        cost_estimate=cost(6 * 10**8, 3 * MB),
        name="last",
    )(back.reshape(SLOTS, D), hidden, gate, flat_col)


def solution(mesh):
    rows = P(AXES, None)
    experts = P(AXES, None, None)
    in_specs = (rows, P(), P(), P(), P(), rows, experts, experts)
    return jax.shard_map(shards, mesh=mesh, in_specs=in_specs, out_specs=rows, check_vma=False)
```

time: 151 us -> 110 us (0.73)
  matrix products: 36.9 us -> 0 us
  Pallas kernels: 0 us -> 26.2 us
  waiting for transfers between devices: 38.7 us -> 19.5 us
  other arithmetic: 16.5 us -> 2.55 us
  blocking collectives: 27.3 us -> 30.7 us
    dot_general x7 -> x0, matrix products: 36.9 us -> none  [the longest x1 10.2 us: shards(): jnp.einsum('hqk,khd->qhd', weights, all_values, preferred_element_type=jn...]
    pallas_call x0 -> x5, Pallas kernels: none -> 26.2 us  [the longest x1 12.8 us: shards(): pl.pallas_call(expert_kernel, out_shape=shape(SLOTS, D), grid=(2, chunks)...]
    ppermute x1, waiting for transfers between devices: 19 us -> 0.01 us  [shards(): halo = lax.ppermute(x[T - LOOK:], AXES, steps)]
    unnamed x38 -> x29, local copies, waits for them, and re-layouts: 1.19 us -> 13.7 us
    convert_element_type x2 -> x0, other arithmetic: 6.23 us -> none  [the longest x1 3.69 us: head_norm(): return scaled.reshape(count, D).astype(jnp.bfloat16)]
    mul x6 -> x2, local copies, waits for them, and re-layouts: 6.07 us -> 0.3 us  [the longest x1 0.15 us: shards(): place = (chosen >> 1) * (2 * CAP) + (chosen & 1)]
    gather x1 -> x0, local copies, waits for them, and re-layouts: 4.65 us -> none  [shards(): picked = returned[flat_index]]
    all_to_all x1, blocking collectives: 27.3 us -> 30.7 us  [shards(): lax.all_to_all(buf.reshape(128, CAP, 2, D), AXES, split_axis=0, concat_ax...]
  transfers between devices with their start and end apart: 2 -> 2, of which waited for: 2 -> 1; matrix products, arithmetic and copies ran while one was open for 2% -> 3% of each run, Pallas kernels for 0% -> 7%
where the time goes in v1:
time: 110 us; the launch traced here: 109 us
  blocking collectives  30.7 us (28%)
  Pallas kernels  26.2 us (24%)
  local copies, waits for them, and re-layouts  20.5 us (19%)
  waiting for transfers between devices  19.5 us (18%)
  starting transfers between devices  9.78 us (9%)
  other arithmetic  2.55 us (2%)
    all_to_all x1, blocking collectives, shards(): lax.all_to_all(buf.reshape(128, CAP, 2, D), AXES, split_axis=0, concat_ax...  30.7 us
    all_to_all x1, waiting for transfers between devices, shards(): lax.all_to_all(out.reshape(128, CAP, 2, D), AXES, split_axis=0, concat_ax...  19.5 us
    unnamed x29, local copies, waits for them, and re-layouts  13.7 us
    pallas_call x1, Pallas kernels, shards(): pl.pallas_call(expert_kernel, out_shape=shape(SLOTS, D), grid=(2, chunks)...  12.8 us
    pallas_call x1, Pallas kernels, shards(): pl.pallas_call(first_kernel, out_shape=(shape(LOOK, D), shape(LOOK, 2 * D...  7.25 us
    all_to_all x1, starting transfers between devices, shards(): lax.all_to_all(out.reshape(128, CAP, 2, D), AXES, split_axis=0, concat_ax...  5.83 us
    ppermute x1, starting transfers between devices, shards(): halo = lax.ppermute(x[T - LOOK:], AXES, steps)  3.95 us
    pallas_call x1, Pallas kernels, shards(): pl.pallas_call(second_kernel, out_shape=(shape(SLOTS, D), shape(T, D), sh...  3.86 us
  transfers between devices with their start and end apart: 2, of which 1 were waited for; matrix products, arithmetic and copies ran while one was open for 3% of the time, Pallas kernels for 7%

profile of v1, /device:TPU:1, one launch (start us, length us, event | category | flops | bytes accessed | tf_op | source)
XLA Modules:
  0.0 109.4 jit_solution(4771177497237831162)
XLA Ops:
  0.0 0.0 copy-start.1
  0.0 0.0 copy-start.13
  0.0 0.0 copy-start.2
  0.0 1.2 %slice.3 = bf16[256,768]{1,0:T(8,128)(2,1)S(1)} slice(bf16[512,768]{1,0:T(8,128)(2,1)} %x_ref.3), slice={[256:512], [0:768]} | slice | bytes 786432 | tf_op jit(solution)/shard_map/slice | solution.py:222
  1.2 3.9 %collective-permute-start = (bf16[256,768]{1,0:T(8,128)(2,1)S(1)}, bf16[256,768]{1,0:T(8,128)(2,1)S(1)}, u32[]{:S(2)}, u32[]{:S(2)}) collective-permute-start(bf16[256,768]{1,0:T(8,128)(2,1)S(1)} %slice.3), channel_id=1, source_target_pairs={{0,1},{1,2},{2,3},{3,4},{4,5},{5,6},{6,7},{7,8},{8,9},{9,10},{10,1... | collective-permute-start | bytes 1179656 | tf_op jit(solution)/shard_map/ppermute | solution.py:222
  5.1 0.7 shift-right-arithmetic_multiply_fusion
  5.8 0.8 copy.26.pick_ref
  6.6 1.1 %convert_reduce_fusion = (s32[512]{0:T(512)S(1)}, s32[512]{0:T(512)S(1)}) fusion(s32[512]{0:T(512)} %bitcast.6), kind=kLoop, calls=%fused_computation.2 | loop fusion | flops 2358272 | bytes 6144 | tf_op jit(solution)/shard_map/reduce_sum | solution.py:228
  7.8 0.1 copy.30
  7.9 0.1 copy.28
  8.1 0.7 fusion
  8.8 0.0 copy-done.13
  8.8 0.1 broadcast_in_dim.2
  8.9 0.1 broadcast_in_dim_reshape.3.scale_ref
  9.0 0.0 copy-done.1
  9.0 0.0 copy-done.2
  9.0 0.0 copy-start
  9.0 2.0 %copy-done = bf16[768,2304]{1,0:T(8,128)(2,1)S(1)} copy-done((bf16[768,2304]{1,0:T(8,128)(2,1)S(1)}, bf16[768,2304]{1,0:T(8,128)(2,1)}, u32[]{:S(2)}) %copy-start) | copy-done | bytes 3538968
  11.0 7.3 %first.1 = (bf16[256,768]{1,0:T(8,128)(2,1)S(1)}, f32[256,1536]{1,0:T(8,128)S(1)}, bf16[256,768]{1,0:T(8,128)(2,1)S(1)}, bf16[256,768]{1,0:T(8,128)(2,1)S(1)}) custom-call(bf16[512,768]{1,0:T(8,128)(2,1)S(1)} %copy-done.1, bf16[768,2304]{1,0:T(8,128)(2,1)S(1)} %copy-done, bf16[768,768]{1,0:T(8,128)(2,1)S(1)} %copy-done.2, ...), custom_call_target="tpu_custom_call" | custom-call | flops 4000000000 | bytes 8388608 | tf_op jit(solution)/shard_map/first/pallas_call | solution.py:232
  18.3 0.0 collective-permute-done.halo_ref
  18.3 0.0 copy-start.8
  18.3 0.7 copy-done.8
  19.0 0.0 copy-start.9
  19.0 1.0 copy-done.9
  20.0 3.9 %second.1 = (bf16[768,768]{1,0:T(8,128)(2,1)S(1)}, bf16[512,768]{1,0:T(8,128)(2,1)S(1)}, bf16[512,768]{1,0:T(8,128)(2,1)S(1)}) custom-call(s32[1]{0:T(128)} %bitcast.valid_ref, bf16[256,768]{1,0:T(8,128)(2,1)S(1)} %copy-done.9, bf16[768,2304]{1,0:T(8,128)(2,1)S(1)} %copy-done, bf16[768,768]{1,0:T(8,128)(2,1)S(1)} %copy-done.2, ...), custom_call_target="tpu_custom_call" | custom-call | flops 2000000000 | bytes 8388608 | tf_op jit(solution)/shard_map/second/pallas_call | solution.py:242
  23.9 0.0 copy-start.4
  23.9 0.9 copy-done.4
  24.8 0.0 copy-start.6
  24.8 0.9 copy-done.6
  25.7 0.5 reshape.70
  26.1 30.7 %all_to_all.10 = bf16[128,3,2,768]{3,2,1,0:T(2,128)(2,1)S(1)} all-to-all(bf16[128,3,2,768]{3,2,1,0:T(2,128)(2,1)S(1)} %reshape.70), channel_id=1, replica_groups=mesh['row'=8,'col'=16] {'row','col'}, dimensions={0} | all-to-all | bytes 2359296 | tf_op jit(solution)/shard_map/all_to_all | solution.py:251
  56.8 0.5 reshape.71.in_ref
  57.3 0.0 copy-start.11
  57.3 3.7 %copy-done.11 = bf16[2,768,3072]{2,1,0:T(8,128)(2,1)S(1)} copy-done((bf16[2,768,3072]{2,1,0:T(8,128)(2,1)S(1)}, bf16[2,768,3072]{2,1,0:T(8,128)(2,1)}, u32[]{:S(2)}) %copy-start.11) | copy-done | bytes 9437208
  61.0 3.7 %copy-done.12 = bf16[2,3072,768]{2,1,0:T(8,128)(2,1)S(1)} copy-done((bf16[2,3072,768]{2,1,0:T(8,128)(2,1)S(1)}, bf16[2,3072,768]{2,1,0:T(8,128)(2,1)}, u32[]{:S(2)}) %copy-start.12) | copy-done | bytes 9437208
  64.7 12.8 %experts.1 = bf16[768,768]{1,0:T(8,128)(2,1)S(1)} custom-call(bf16[768,768]{1,0:T(8,128)(2,1)S(1)} %reshape.71.in_ref, bf16[2,768,3072]{2,1,0:T(8,128)(2,1)S(1)} %copy-done.11, bf16[2,3072,768]{2,1,0:T(8,128)(2,1)S(1)} %copy-done.12), custom_call_target="tpu_custom_call" | custom-call | flops 7000000000 | bytes 20971520 | tf_op jit(solution)/shard_map/experts/pallas_call | solution.py:254
  77.5 1.3 %reshape.72 = bf16[128,3,2,768]{3,2,1,0:T(2,128)(2,1)} reshape(bf16[768,768]{1,0:T(8,128)(2,1)S(1)} %experts.1) | data formatting | bytes 2359296 | tf_op jit(solution)/shard_map/reshape | solution.py:269
  78.8 5.8 %all-to-all-start.1 = ((bf16[128,3,2,768]{3,2,1,0:T(2,128)(2,1)}), bf16[128,3,2,768]{3,2,1,0:T(2,128)(2,1)}, u32[]{:S(2)}, u32[]{:S(2)}) async-start(bf16[128,3,2,768]{3,2,1,0:T(2,128)(2,1)} %reshape.72), calls=%async_computation.1 | async-start | bytes 2359296 | tf_op jit(solution)/shard_map/all_to_all | solution.py:269
  84.6 0.0 copy-done.7
  84.6 0.0 copy-done.10
  84.7 0.5 gate.1.gate_ref
  85.1 0.0 copy-start.3
  85.1 0.0 copy-start.5
  85.1 19.5 %all-to-all-done.1 = bf16[128,3,2,768]{3,2,1,0:T(2,128)(2,1)} async-done(((bf16[128,3,2,768]{3,2,1,0:T(2,128)(2,1)}), bf16[128,3,2,768]{3,2,1,0:T(2,128)(2,1)}, u32[]{:S(2)}, u32[]{:S(2)}) %all-to-all-start.1) | async-done | bytes 1179680 | tf_op jit(solution)/shard_map/all_to_all | solution.py:269
  104.7 3.0 %reshape.73.back_ref = bf16[768,768]{1,0:T(8,128)(2,1)S(1)} reshape(bf16[128,3,2,768]{3,2,1,0:T(2,128)(2,1)} %all-to-all-done.1) | data formatting | bytes 2359296 | tf_op jit(solution)/shard_map/reshape | solution.py:283
  107.6 0.0 copy-done.3
  107.7 0.0 copy-done.5
  107.7 1.7 %last.1 = bf16[512,768]{1,0:T(8,128)(2,1)} custom-call(bf16[768,768]{1,0:T(8,128)(2,1)S(1)} %reshape.73.back_ref, bf16[512,768]{1,0:T(8,128)(2,1)S(1)} %copy-done.5, f32[512,1]{1,0:T(8,128)S(1)} %gate.1.gate_ref, s32[512,1]{1,0:T(8,128)S(1)} %copy-done.3), custom_call_target="tpu_custom_call" | custom-call | flops 600000000 | bytes 3145728 | tf_op jit(solution)/shard_map/last/pallas_call | solution.py:277
  (6 shorter events, 0.0 us)
Async XLA Ops:
  0.0 9.0 %copy-start.1 = (bf16[512,768]{1,0:T(8,128)(2,1)S(1)}, bf16[512,768]{1,0:T(8,128)(2,1)}, u32[]{:S(2)}) copy-start(bf16[512,768]{1,0:T(8,128)(2,1)} %x_ref.3) | copy-start | bytes 2359300
  0.0 8.8 %copy-start.13 = (f32[12]{0:T(128)S(1)}, f32[12]{0:T(128)}, u32[]{:S(2)}) copy-start(f32[12]{0:T(128)} %param.11) | copy-start | bytes 148
  0.0 9.0 %copy-start.2 = (bf16[768,768]{1,0:T(8,128)(2,1)S(1)}, bf16[768,768]{1,0:T(8,128)(2,1)}, u32[]{:S(2)}) copy-start(bf16[768,768]{1,0:T(8,128)(2,1)} %mix_ref.3) | copy-start | bytes 3538948
  1.2 17.1 %collective-permute-start = (bf16[256,768]{1,0:T(8,128)(2,1)S(1)}, bf16[256,768]{1,0:T(8,128)(2,1)S(1)}, u32[]{:S(2)}, u32[]{:S(2)}) collective-permute-start(bf16[256,768]{1,0:T(8,128)(2,1)S(1)} %slice.3), channel_id=1, source_target_pairs={{0,1},{1,2},{2,3},{3,4},{4,5},{5,6},{6,7},{7,8},{8,9},{9,10},{10,1... | collective-permute-start | bytes 1179656 | tf_op jit(solution)/shard_map/ppermute | solution.py:222
  9.0 2.0 %copy-start = (bf16[768,2304]{1,0:T(8,128)(2,1)S(1)}, bf16[768,2304]{1,0:T(8,128)(2,1)}, u32[]{:S(2)}) copy-start(bf16[768,2304]{1,0:T(8,128)(2,1)} %w_ref.3) | copy-start | bytes 10616836
  18.3 0.7 copy-start.8
  19.0 1.0 copy-start.9
  23.9 0.9 copy-start.4
  24.8 0.9 copy-start.6
  57.3 3.7 %copy-start.11 = (bf16[2,768,3072]{2,1,0:T(8,128)(2,1)S(1)}, bf16[2,768,3072]{2,1,0:T(8,128)(2,1)}, u32[]{:S(2)}) copy-start(bf16[2,768,3072]{2,1,0:T(8,128)(2,1)} %first_ref.1) | copy-start | bytes 28311556
  61.0 3.7 %copy-start.12 = (bf16[2,3072,768]{2,1,0:T(8,128)(2,1)S(1)}, bf16[2,3072,768]{2,1,0:T(8,128)(2,1)}, u32[]{:S(2)}) copy-start(bf16[2,3072,768]{2,1,0:T(8,128)(2,1)} %second_ref.1) | copy-start | bytes 28311556
  78.8 5.8 %copy-start.7 = (bf16[512,768]{1,0:T(8,128)(2,1)S(1)}, bf16[512,768]{1,0:T(8,128)(2,1)}, u32[]{:S(2)}) copy-start(bf16[512,768]{1,0:T(8,128)(2,1)} %copy-done.6) | copy-start | bytes 2359300
  78.8 5.8 %copy-start.10 = (bf16[768,256]{1,0:T(8,128)(2,1)S(1)}, bf16[768,256]{1,0:T(8,128)(2,1)}, u32[]{:S(2)}) copy-start(bf16[768,256]{1,0:T(8,128)(2,1)} %columns_ref.1) | copy-start | bytes 1179652
  78.8 25.9 %all-to-all-start.1 = ((bf16[128,3,2,768]{3,2,1,0:T(2,128)(2,1)}), bf16[128,3,2,768]{3,2,1,0:T(2,128)(2,1)}, u32[]{:S(2)}, u32[]{:S(2)}) async-start(bf16[128,3,2,768]{3,2,1,0:T(2,128)(2,1)} %reshape.72), calls=%async_computation.1 | async-start | bytes 2359296 | tf_op jit(solution)/shard_map/all_to_all | solution.py:269
  85.1 22.5 %copy-start.3 = (s32[512,1]{1,0:T(8,128)S(1)}, s32[512,1]{1,0:T(8,128)}, u32[]{:S(2)}) copy-start(s32[512,1]{1,0:T(8,128)} %get-tuple-element.21.col_ref) | copy-start | bytes 6148
  85.1 22.5 %copy-start.5 = (bf16[512,768]{1,0:T(8,128)(2,1)S(1)}, bf16[512,768]{1,0:T(8,128)(2,1)}, u32[]{:S(2)}) copy-start(bf16[512,768]{1,0:T(8,128)(2,1)} %copy-done.4) | copy-start | bytes 2359300

commit v2 on v1

v2 whole, which is shorter than its diff:
```python
import math

import jax
import jax.numpy as jnp
from jax import lax
from jax.experimental import pallas as pl
from jax.experimental.pallas import tpu as pltpu
from jax.sharding import PartitionSpec as P

D = 768
HEADS = 12
LOOK = 256
T = 512
FF = 3072
CAP = 3
SLOTS = 768
PAIRS = HEADS // 2
LANES = 128
AXES = ("row", "col")
BF = jnp.bfloat16
F32 = jnp.float32
MB = 1 << 20


def dot(a, b):
    return jnp.dot(a, b, preferred_element_type=F32)


def dot_t(a, b):
    return lax.dot_general(a, b, (((1,), (1,)), ((), ())), preferred_element_type=F32)


def norm_rows(value):
    center = value - jnp.mean(value, axis=-1, keepdims=True)
    spread = jnp.mean(center * center, axis=-1, keepdims=True)
    return (center * lax.rsqrt(spread + 1e-05)).astype(BF)


def head_blocks():
    down = lax.shift_right_logical(lax.broadcasted_iota(jnp.int32, (256, 256), 0), 6)
    across = lax.shift_right_logical(lax.broadcasted_iota(jnp.int32, (256, 256), 1), 6)
    return jnp.where(down == across, 1.0, 0.0).astype(BF)


def head_norm(value, blocks):
    square = (value * value).astype(BF)
    return value * lax.rsqrt(dot(square, blocks) * (1.0 / 64) + 1e-06)


def triangles():
    down = lax.broadcasted_iota(jnp.int32, (128, 128), 0)
    across = lax.broadcasted_iota(jnp.int32, (128, 128), 1)
    behind = jnp.where(across >= down, 1.0, 0.0).astype(BF)
    ahead = jnp.where(across <= down, 1.0, 0.0).astype(BF)
    return behind, ahead


def half_lanes(half):
    lane = lax.broadcasted_iota(jnp.int32, (1, LANES), 1)
    mine = (lane < 64) if half == 0 else (lane >= 64)
    return jnp.where(mine, 1.0, 0.0).astype(BF)


def weigh(part):
    return jnp.exp2(part).astype(BF)


def behind_weights(scores, behind):
    top = jnp.concatenate([weigh(scores[:128, :128]) * behind, weigh(scores[:128, 128:])], axis=1)
    low = jnp.concatenate([jnp.zeros((128, 128), BF), weigh(scores[128:, 128:]) * behind], axis=1)
    return jnp.concatenate([top, low], axis=0)


def own_weights(scores, ahead):
    top = jnp.concatenate([weigh(scores[:128, :128]) * ahead, jnp.zeros((128, 128), BF)], axis=1)
    low = jnp.concatenate([weigh(scores[128:, :128]), weigh(scores[128:, 128:]) * ahead], axis=1)
    return jnp.concatenate([top, low], axis=0)


def payload(values, half, ones):
    mask = half_lanes(half)
    return jnp.concatenate([values * mask, ones * mask], axis=1)


def norm_into(source, target, count):
    def step(i, carry):
        r = pl.ds(pl.multiple_of(i * 64, 64), 64)
        target[r, :] = norm_rows(source[r, :].astype(F32))
        return carry

    lax.fori_loop(0, count // 64, step, 0)


def scale_lanes(scale_ref, group):
    lane = lax.broadcasted_iota(jnp.int32, (1, 256), 1)
    value = jnp.full((1, 256), scale_ref[4 * group], F32)
    for h in range(1, 4):
        value = jnp.where(lane >= 64 * h, scale_ref[4 * group + h], value)
    return value * (math.log2(math.e) / 64)


def places(row_ref, flat_out, wide_out, pick_s):
    row = row_ref[...]
    rowf = row.astype(F32)
    rowb = jnp.broadcast_to(rowf, (LANES, T)).astype(BF)
    for r in range(0, T, 128):
        down = lax.broadcasted_iota(jnp.int32, (128, T), 0) + r
        across = lax.broadcasted_iota(jnp.int32, (128, T), 1)
        eye = jnp.where(down == across, 1.0, 0.0).astype(BF)
        wide = dot_t(eye, rowb)
        pick_s[r : r + 128, :] = wide.astype(jnp.int32)
        same = (jnp.concatenate([wide] * 4, axis=1) == rowf) & (across < down)
        same = jnp.where(same, 1.0, 0.0).astype(BF)
        slot = dot(same, jnp.ones((T, LANES), BF)).astype(jnp.int32)
        mine = pick_s[r : r + 128, :]
        wide_out[r : r + 128, :] = (mine >> 1) * (2 * CAP) + (mine & 1) + 2 * slot
        slot_row = dot_t(jnp.ones((8, T), BF), same)[:1].astype(jnp.int32)
        part = row[:, r : r + 128]
        flat_out[:, r : r + 128] = (part >> 1) * (2 * CAP) + (part & 1) + 2 * slot_row


def gates(routed, columns, pick):
    logits = dot(routed, columns)
    lane = lax.broadcasted_iota(jnp.int32, (1, LANES), 1)
    kept = jnp.where(pick == lane, logits[:, :LANES], 0.0) + jnp.where(pick == lane + LANES, logits[:, LANES:], 0.0)
    return 1.0 / (1.0 + jnp.exp(-jnp.sum(kept, axis=1, keepdims=True)))


def finish(ctx, mix_ref, x_ref, x_at, columns_ref, pick_ref, hid_out, rou_out, gate_out):
    for r in range(0, LOOK, 128):
        mixed = dot(ctx[r : r + 128, :], mix_ref[...])
        for s in range(r, r + 128, 32):
            hidden = (x_ref[x_at + s : x_at + s + 32, :].astype(F32) + mixed[s - r : s - r + 32, :]).astype(BF)
            hid_out[s : s + 32, :] = hidden
            rou_out[s : s + 32, :] = norm_rows(hidden.astype(F32))
        gate_out[r : r + 128, :] = gates(rou_out[r : r + 128, :], columns_ref[...], pick_ref[x_at + r : x_at + r + 128, :])


def first_kernel(
    scale_hbm, x_hbm, w_hbm, mix_hbm, columns_hbm, row_hbm,
    q_out, acc_out, hid_out, rou_out, gate_out, flat_out, wide_out, pick_out, x_ref, kv_out, mix_ref, columns_ref,
    normed, wq, q_s, k_s, v_s, ctx, row_ref, scale_ref, sems,
):
    fetch = pltpu.make_async_copy(x_hbm, x_ref, sems.at[0])
    copies = [
        pltpu.make_async_copy(w_hbm.at[:, pl.ds(0, D)], wq, sems.at[1]),
        pltpu.make_async_copy(w_hbm.at[:, pl.ds(D, 2 * D)], kv_out, sems.at[2]),
        pltpu.make_async_copy(columns_hbm, columns_ref, sems.at[3]),
        pltpu.make_async_copy(mix_hbm, mix_ref, sems.at[4]),
        pltpu.make_async_copy(row_hbm, row_ref, sems.at[5]),
        pltpu.make_async_copy(scale_hbm, scale_ref, sems.at[6]),
    ]
    fetch.start()
    for copy in copies:
        copy.start()
    fetch.wait()
    norm_into(x_ref, normed, T)
    for copy in copies:
        copy.wait()
    places(row_ref, flat_out, wide_out, pick_out)
    blocks = head_blocks()
    for g in range(3):
        c = slice(g * 256, g * 256 + 256)
        value = head_norm(dot(normed[...], wq[:, c]), blocks)
        q_s[:, c] = (value * scale_lanes(scale_ref, g)).astype(BF)
        k_s[:, c] = head_norm(dot(normed[...], kv_out[:, c]), blocks).astype(BF)
        v_s[:, c] = dot(normed[...], kv_out[:, D + g * 256 : D + g * 256 + 256]).astype(BF)
    q_out[...] = q_s[:LOOK, :]
    behind, ahead = triangles()
    ones = jnp.ones((LOOK, LANES), BF)
    for pair in range(PAIRS):
        c = slice(pair * LANES, pair * LANES + LANES)
        low = jnp.zeros((LOOK, 256), F32)
        high = jnp.zeros((LOOK, 256), F32)
        for half in range(2):
            mask = half_lanes(half)
            q0 = q_s[:LOOK, c] * mask
            q1 = q_s[LOOK:, c] * mask
            k0 = k_s[:LOOK, c]
            k1 = k_s[LOOK:, c]
            v0 = payload(v_s[:LOOK, c], half, ones)
            v1 = payload(v_s[LOOK:, c], half, ones)
            low += dot(own_weights(dot_t(q0, k0), ahead), v0)
            high += dot(behind_weights(dot_t(q1, k0), behind), v0)
            high += dot(own_weights(dot_t(q1, k1), ahead), v1)
        acc_out[:, pair * 256 : pair * 256 + 256] = low
        ctx[:, c] = (high[:, :LANES] / high[:, LANES:]).astype(BF)
    finish(ctx, mix_ref, x_ref, LOOK, columns_ref, pick_out, hid_out, rou_out, gate_out)


def second_kernel(
    valid_ref, halo_ref, kv_ref, mix_ref, x_ref, columns_ref, q_ref, acc_ref, rou_ref, row_ref, pick_ref,
    buf_out, hid_out, gate_out, normed, k_s, v_s, ctx, routed,
):
    for r in range(0, LOOK, 32):
        normed[r : r + 32, :] = norm_rows(halo_ref[r : r + 32, :].astype(F32))
    blocks = head_blocks()
    for g in range(3):
        c = slice(g * 256, g * 256 + 256)
        k_s[:, c] = head_norm(dot(normed[...], kv_ref[:, c]), blocks).astype(BF)
        v_s[:, c] = dot(normed[...], kv_ref[:, D + g * 256 : D + g * 256 + 256]).astype(BF)
    behind, _ = triangles()
    ones = jnp.full((LOOK, LANES), valid_ref[0].astype(F32)).astype(BF)
    for pair in range(PAIRS):
        c = slice(pair * LANES, pair * LANES + LANES)
        low = acc_ref[:, pair * 256 : pair * 256 + 256]
        for half in range(2):
            q0 = q_ref[:, c] * half_lanes(half)
            low += dot(behind_weights(dot_t(q0, k_s[:, c]), behind), payload(v_s[:, c] * ones, half, ones))
        ctx[:, c] = (low[:, :LANES] / low[:, LANES:]).astype(BF)
    finish(ctx, mix_ref, x_ref, 0, columns_ref, pick_ref, hid_out, routed, gate_out)
    for s in range(0, SLOTS, 256):
        place = lax.broadcasted_iota(jnp.int32, (256, T), 0) + s
        pick = jnp.where(place == row_ref[...], 1.0, 0.0).astype(BF)
        rows = dot(pick[:, :LOOK], routed[...]) + dot(pick[:, LOOK:], rou_ref[...])
        buf_out[s // 2 : s // 2 + 128] = rows.astype(BF).reshape(128, 2, D)


def take_rows(expert):
    down = lax.broadcasted_iota(jnp.int32, (128, 256), 0)
    across = lax.broadcasted_iota(jnp.int32, (128, 256), 1)
    return jnp.where(across == 2 * down + expert, 1.0, 0.0).astype(BF)


def put_rows(expert):
    down = lax.broadcasted_iota(jnp.int32, (256, 128), 0)
    across = lax.broadcasted_iota(jnp.int32, (256, 128), 1)
    return jnp.where(down == 2 * across + expert, 1.0, 0.0).astype(BF)


def expert_kernel(in_ref, first_ref, second_ref, out_ref, rows, hidden, done):
    arrived = in_ref[...].reshape(SLOTS, D)
    for e in range(2):
        pick = take_rows(e)
        for b in range(3):
            rows[e, b * 128 : b * 128 + 128, :] = dot(pick, arrived[b * 256 : b * 256 + 256, :]).astype(BF)
    for e in range(2):
        for s in range(0, FF, 768):
            hidden[:, s : s + 768] = jnp.maximum(dot(rows[e], first_ref[e, :, s : s + 768]), 0.0).astype(BF)
        done[e] = dot(hidden[...], second_ref[e]).astype(BF)
    for b in range(3):
        r = slice(b * 128, b * 128 + 128)
        mixed = dot(put_rows(0), done[0, r, :]) + dot(put_rows(1), done[1, r, :])
        out_ref[r] = mixed.astype(BF).reshape(128, 2, D)


def last_kernel(back_ref, hid0_ref, hid1_ref, gate0_ref, gate1_ref, wide_ref, out_ref):
    back = back_ref[...].reshape(SLOTS, D)
    for r, hid_ref, gate_ref in ((0, hid0_ref, gate0_ref), (LOOK, hid1_ref, gate1_ref)):
        across = lax.broadcasted_iota(jnp.int32, (LOOK, SLOTS), 1)
        place = jnp.concatenate([wide_ref[r : r + LOOK, :]] * 6, axis=1)
        pick = jnp.where(across == place, 1.0, 0.0).astype(BF)
        picked = dot(pick, back)
        out_ref[r : r + LOOK, :] = (hid_ref[...].astype(F32) + gate_ref[...] * picked).astype(BF)


def params(limit):
    return pltpu.CompilerParams(vmem_limit_bytes=limit * MB)


def shape(*dims, dtype=BF):
    return jax.ShapeDtypeStruct(dims, dtype)


def cost(flops, moved, exps=0):
    return pl.CostEstimate(flops=flops, bytes_accessed=moved, transcendentals=exps)


def far(value):
    return pltpu.with_memory_space_constraint(value, pltpu.HBM)


def shards(x, triple, mixing, scaling, columns, pick, entry, exits):
    steps = [(i, i + 1) for i in range(127)]
    halo = lax.ppermute(x[T - LOOK :], AXES, steps)
    row = pick.reshape(1, T)
    vmem = pl.BlockSpec(memory_space=pltpu.VMEM)
    smem = pl.BlockSpec(memory_space=pltpu.SMEM)
    hbm = pl.BlockSpec(memory_space=pltpu.HBM)
    q0, acc0, hid1, rou1, gate1, flat, wide, chosen, x_near, kv, mix_near, columns_near = pl.pallas_call(
        first_kernel,
        out_shape=(
            shape(LOOK, D),
            shape(LOOK, 2 * D, dtype=F32),
            shape(LOOK, D),
            shape(LOOK, D),
            shape(LOOK, 1, dtype=F32),
            shape(1, T, dtype=jnp.int32),
            shape(T, LANES, dtype=jnp.int32),
            shape(T, LANES, dtype=jnp.int32),
            shape(T, D),
            shape(D, 2 * D),
            shape(D, D),
            shape(D, 256),
        ),
        in_specs=[hbm] * 6,
        out_specs=(vmem,) * 12,
        scratch_shapes=[pltpu.VMEM((T, D), BF), pltpu.VMEM((D, D), BF)]
        + [pltpu.VMEM((T, D), BF)] * 3
        + [
            pltpu.VMEM((LOOK, D), BF),
            pltpu.VMEM((1, T), jnp.int32),
            pltpu.SMEM((HEADS,), F32),
            pltpu.SemaphoreType.DMA((7,)),
        ],
        compiler_params=params(16),
        cost_estimate=cost(4 * 10**9, 8 * MB),
        name="first",
    )(*(far(a) for a in (scaling, x, triple, mixing, columns, row)))
    valid = jnp.minimum(lax.axis_index(AXES), 1).astype(jnp.int32).reshape(1)
    buf, hid0, gate0 = pl.pallas_call(
        second_kernel,
        out_shape=(shape(SLOTS // 2, 2, D), shape(LOOK, D), shape(LOOK, 1, dtype=F32)),
        in_specs=[smem] + [vmem] * 10,
        out_specs=(vmem,) * 3,
        scratch_shapes=[pltpu.VMEM((LOOK, D), BF)] * 5,
        compiler_params=params(16),
        cost_estimate=cost(2 * 10**9, 8 * MB),
        name="second",
    )(valid, halo, kv, mix_near, x_near, columns_near, q0, acc0, rou1, flat, chosen)
    arrived = lax.all_to_all(buf.reshape(128, CAP, 2, D), AXES, split_axis=0, concat_axis=0, tiled=True)
    out = pl.pallas_call(
        expert_kernel,
        out_shape=shape(SLOTS // 2, 2, D),
        scratch_shapes=[pltpu.VMEM((2, SLOTS // 2, D), BF), pltpu.VMEM((SLOTS // 2, FF), BF), pltpu.VMEM((2, SLOTS // 2, D), BF)],
        compiler_params=params(14),
        cost_estimate=cost(7 * 10**9, 20 * MB),
        name="experts",
    )(arrived.reshape(SLOTS // 2, 2, D), entry, exits)
    back = lax.all_to_all(out.reshape(128, CAP, 2, D), AXES, split_axis=0, concat_axis=0, tiled=True)
    return pl.pallas_call(
        last_kernel,
        out_shape=shape(T, D),
        compiler_params=params(16),
        cost_estimate=cost(6 * 10**8, 3 * MB),
        name="last",
    )(back.reshape(SLOTS // 2, 2, D), hid0, hid1, gate0, gate1, wide)


def solution(mesh):
    rows = P(AXES, None)
    experts = P(AXES, None, None)
    in_specs = (rows, P(), P(), P(), P(), rows, experts, experts)
    return jax.shard_map(shards, mesh=mesh, in_specs=in_specs, out_specs=rows, check_vma=False)
```

time: 110 us -> 87.4 us (0.79)
  blocking collectives: 30.7 us -> 53.6 us
  local copies, waits for them, and re-layouts: 20.5 us -> 1.04 us
  waiting for transfers between devices: 19.5 us -> 1.67 us
  starting transfers between devices: 9.78 us -> 3.95 us
  other arithmetic: 2.55 us -> 0.01 us
    all_to_all x0 -> x1, blocking collectives: none -> 24.5 us  [shards(): lax.all_to_all(out.reshape(128, CAP, 2, D), AXES, split_axis=0, concat_ax...]
    all_to_all x1 -> x0, waiting for transfers between devices: 19.5 us -> none  [shards(): lax.all_to_all(out.reshape(128, CAP, 2, D), AXES, split_axis=0, concat_ax...]
    unnamed x29 -> x8, local copies, waits for them, and re-layouts: 13.7 us -> 0.02 us
    all_to_all x1 -> x0, starting transfers between devices: 5.83 us -> none  [shards(): lax.all_to_all(out.reshape(128, CAP, 2, D), AXES, split_axis=0, concat_ax...]
    reshape x4 -> x0, local copies, waits for them, and re-layouts: 5.18 us -> none  [the longest x1 2.95 us: shards(): back.reshape(SLOTS, D)]
    pallas_call x1, Pallas kernels: 7.25 us -> 11.3 us  [shards(): pl.pallas_call(first_kernel, out_shape=(shape(LOOK, D), shape(LOOK, 2 * D...]
    pallas_call x3 -> x2, Pallas kernels: 17.2 us -> 13.8 us  [the longest x1 9.61 us: shards(): pl.pallas_call(expert_kernel, out_shape=shape(SLOTS // 2, 2, D), scratch_...]
    ppermute x1, waiting for transfers between devices: 0.01 us -> 1.67 us  [shards(): halo = lax.ppermute(x[T - LOOK:], AXES, steps)]
  transfers between devices with their start and end apart: 2 -> 1, of which waited for: 1 -> 1; matrix products, arithmetic and copies ran while one was open for 3% -> 0% of each run, Pallas kernels for 7% -> 13%
where the time goes in v2:
time: 87.4 us; the launch traced here: 87.2 us
  blocking collectives  53.6 us (61%)
  Pallas kernels  26.8 us (31%)
  starting transfers between devices  3.95 us (5%)
  waiting for transfers between devices  1.67 us (2%)
  local copies, waits for them, and re-layouts  1.04 us (1%)
    all_to_all x1, blocking collectives, shards(): lax.all_to_all(buf.reshape(128, CAP, 2, D), AXES, split_axis=0, concat_ax...  29 us
    all_to_all x1, blocking collectives, shards(): lax.all_to_all(out.reshape(128, CAP, 2, D), AXES, split_axis=0, concat_ax...  24.5 us
    pallas_call x1, Pallas kernels, shards(): pl.pallas_call(first_kernel, out_shape=(shape(LOOK, D), shape(LOOK, 2 * D...  11.3 us
    pallas_call x1, Pallas kernels, shards(): pl.pallas_call(expert_kernel, out_shape=shape(SLOTS // 2, 2, D), scratch_...  9.61 us
    pallas_call x1, Pallas kernels, shards(): pl.pallas_call(second_kernel, out_shape=(shape(SLOTS // 2, 2, D), shape(L...  4.18 us
    ppermute x1, starting transfers between devices, shards(): halo = lax.ppermute(x[T - LOOK:], AXES, steps)  3.95 us
  transfers between devices with their start and end apart: 1, of which 1 were waited for; matrix products, arithmetic and copies ran while one was open for 0% of the time, Pallas kernels for 13%

profile of v2, /device:TPU:1, one launch (start us, length us, event | category | flops | bytes accessed | tf_op | source)
XLA Modules:
  0.0 87.2 jit_solution(16028125294389468321)
XLA Ops:
  0.0 1.0 %slice.3 = bf16[256,768]{1,0:T(8,128)(2,1)S(1)} slice(bf16[512,768]{1,0:T(8,128)(2,1)} %x_hbm.1), slice={[256:512], [0:768]} | slice | bytes 786432 | tf_op jit(solution)/shard_map/slice | solution.py:275
  1.0 3.9 %collective-permute-start = (bf16[256,768]{1,0:T(8,128)(2,1)S(1)}, bf16[256,768]{1,0:T(8,128)(2,1)S(1)}, u32[]{:S(2)}, u32[]{:S(2)}) collective-permute-start(bf16[256,768]{1,0:T(8,128)(2,1)S(1)} %slice.3), channel_id=1, source_target_pairs={{0,1},{1,2},{2,3},{3,4},{4,5},{5,6},{6,7},{7,8},{8,9},{9,10},{10,1... | collective-permute-start | bytes 1179656 | tf_op jit(solution)/shard_map/ppermute | solution.py:275
  5.0 0.0 slice-start
  5.0 0.0 slice-start.1
  5.0 0.0 copy-start
  5.0 11.3 %first.1 = (bf16[256,768]{1,0:T(8,128)(2,1)S(1)}, f32[256,1536]{1,0:T(8,128)S(1)}, bf16[256,768]{1,0:T(8,128)(2,1)S(1)}, bf16[256,768]{1,0:T(8,128)(2,1)S(1)}, f...) custom-call(f32[12]{0:T(128)} %scale_hbm.1, ...), custom_call_target="tpu_custom_call" | custom-call | flops 4000000000 | bytes 8388608 | tf_op jit(solution)/shard_map/first/pallas_call | solution.py:280
  16.4 1.7 %collective-permute-done.halo_ref = bf16[256,768]{1,0:T(8,128)(2,1)S(1)} collective-permute-done((bf16[256,768]{1,0:T(8,128)(2,1)S(1)}, bf16[256,768]{1,0:T(8,128)(2,1)S(1)}, u32[]{:S(2)}, u32[]{:S(2)}) %collective-permute-start) | collective-permute-done | bytes 393248 | tf_op jit(solution)/shard_map/ppermute | solution.py:275
  18.0 0.0 slice-start.2
  18.0 4.2 %second.1 = (bf16[384,2,768]{2,1,0:T(2,128)(2,1)S(1)}, bf16[256,768]{1,0:T(8,128)(2,1)S(1)}, f32[256,1]{1,0:T(8,128)S(1)}) custom-call(s32[1]{0:T(128)} %bitcast.valid_ref, bf16[256,768]{1,0:T(8,128)(2,1)S(1)} %collective-permute-done.halo_ref, bf16[768,1536]{1,0:T(8,128)(2,1)S(1)} %get-tuple-element.20.kv_ref, ...), custom_call_target="tpu_custom_call" | custom-call | flops 2000000000 | bytes 8388608 | tf_op jit(solution)/shard_map/second/pallas_call | solution.py:311
  22.2 29.0 %all_to_all.10 = bf16[128,3,2,768]{3,2,1,0:T(2,128)(2,1)S(1)} all-to-all(bf16[128,3,2,768]{3,2,1,0:T(2,128)(2,1)S(1)} %bitcast.7), channel_id=1, replica_groups=mesh['row'=8,'col'=16] {'row','col'}, dimensions={0} | all-to-all | bytes 2359296 | tf_op jit(solution)/shard_map/all_to_all | solution.py:321
  51.3 0.0 slice-done
  51.3 0.0 slice-done.1
  51.3 0.0 copy-done
  51.3 0.0 slice-done.2
  51.3 9.6 %experts.1 = bf16[384,2,768]{2,1,0:T(2,128)(2,1)S(1)} custom-call(bf16[384,2,768]{2,1,0:T(2,128)(2,1)S(1)} %bitcast.8, bf16[2,768,3072]{2,1,0:T(8,128)(2,1)S(1)} %bitcast.11, bf16[2,3072,768]{2,1,0:T(8,128)(2,1)S(1)} %copy-done), custom_call_target="tpu_custom_call" | custom-call | flops 7000000000 | bytes 20971520 | tf_op jit(solution)/shard_map/experts/pallas_call | solution.py:322
  60.9 24.5 %all_to_all.11 = bf16[128,3,2,768]{3,2,1,0:T(2,128)(2,1)S(1)} all-to-all(bf16[128,3,2,768]{3,2,1,0:T(2,128)(2,1)S(1)} %bitcast.9), channel_id=1, replica_groups=mesh['row'=8,'col'=16] {'row','col'}, dimensions={0} | all-to-all | bytes 2359296 | tf_op jit(solution)/shard_map/all_to_all | solution.py:330
  85.4 1.7 %last.1 = bf16[512,768]{1,0:T(8,128)(2,1)} custom-call(bf16[384,2,768]{2,1,0:T(2,128)(2,1)S(1)} %bitcast.6, bf16[256,768]{1,0:T(8,128)(2,1)S(1)} %get-tuple-element.30.hid0_ref, bf16[256,768]{1,0:T(8,128)(2,1)S(1)} %get-tuple-element.31.hid1_ref, f32[256,1]{1,0:T(8,128)S(1)} %get-tuple-element.32.gate0_ref, f32[256,1]{1,0:T(8,128)S(1)} %get-tuple-element.33.gate1_ref, ...), custom_call_target="tpu_custom_call" | custom-call | flops 600000000 | bytes 3145728 | tf_op jit(solution)/shard_map/last/pallas_call | solution.py:331
  (1 shorter events, 0.0 us)
Async XLA Ops:
  1.0 17.0 %collective-permute-start = (bf16[256,768]{1,0:T(8,128)(2,1)S(1)}, bf16[256,768]{1,0:T(8,128)(2,1)S(1)}, u32[]{:S(2)}, u32[]{:S(2)}) collective-permute-start(bf16[256,768]{1,0:T(8,128)(2,1)S(1)} %slice.3), channel_id=1, source_target_pairs={{0,1},{1,2},{2,3},{3,4},{4,5},{5,6},{6,7},{7,8},{8,9},{9,10},{10,1... | collective-permute-start | bytes 1179656 | tf_op jit(solution)/shard_map/ppermute | solution.py:275
  5.0 46.3 %slice-start = ((s8[9437184]{0:T(1024)(128)(4,1)}), s8[4194304]{0:T(1024)(128)(4,1)S(1)}, s32[]{:S(2)}) async-start(s8[9437184]{0:T(1024)(128)(4,1)} %bitcast.10), calls=%async_computation.2 | async-start | bytes 8388608
  5.0 46.3 %slice-start.1 = ((s8[9437184]{0:T(1024)(128)(4,1)}), s8[4194304]{0:T(1024)(128)(4,1)S(1)}, s32[]{:S(2)}) async-start(s8[9437184]{0:T(1024)(128)(4,1)} %bitcast.10), calls=%async_computation.3 | async-start | bytes 8388608
  5.0 46.3 %copy-start = (bf16[2,3072,768]{2,1,0:T(8,128)(2,1)S(1)}, bf16[2,3072,768]{2,1,0:T(8,128)(2,1)}, u32[]{:S(2)}) copy-start(bf16[2,3072,768]{2,1,0:T(8,128)(2,1)} %second_ref.1) | copy-start | bytes 28311556
  18.0 33.2 %slice-start.2 = ((s8[9437184]{0:T(1024)(128)(4,1)}), s8[1048576]{0:T(1024)(128)(4,1)S(1)}, s32[]{:S(2)}) async-start(s8[9437184]{0:T(1024)(128)(4,1)} %bitcast.10), calls=%async_computation.4 | async-start | bytes 2097152

commit v3 on v2

--- a/solution.py
+++ b/solution.py
@@ -99,7 +99,7 @@
     return value * (math.log2(math.e) / 64)
 
 
-def places(row_ref, flat_out, wide_out, pick_s):
+def places(row_ref, flat_out, wide_out):
     row = row_ref[...]
     rowf = row.astype(F32)
     rowb = jnp.broadcast_to(rowf, (LANES, T)).astype(BF)
@@ -108,38 +108,54 @@
         across = lax.broadcasted_iota(jnp.int32, (128, T), 1)
         eye = jnp.where(down == across, 1.0, 0.0).astype(BF)
         wide = dot_t(eye, rowb)
-        pick_s[r : r + 128, :] = wide.astype(jnp.int32)
         same = (jnp.concatenate([wide] * 4, axis=1) == rowf) & (across < down)
         same = jnp.where(same, 1.0, 0.0).astype(BF)
         slot = dot(same, jnp.ones((T, LANES), BF)).astype(jnp.int32)
-        mine = pick_s[r : r + 128, :]
+        mine = wide.astype(jnp.int32)
         wide_out[r : r + 128, :] = (mine >> 1) * (2 * CAP) + (mine & 1) + 2 * slot
         slot_row = dot_t(jnp.ones((8, T), BF), same)[:1].astype(jnp.int32)
         part = row[:, r : r + 128]
         flat_out[:, r : r + 128] = (part >> 1) * (2 * CAP) + (part & 1) + 2 * slot_row
 
 
-def gates(routed, columns, pick):
-    logits = dot(routed, columns)
-    lane = lax.broadcasted_iota(jnp.int32, (1, LANES), 1)
-    kept = jnp.where(pick == lane, logits[:, :LANES], 0.0) + jnp.where(pick == lane + LANES, logits[:, LANES:], 0.0)
-    return 1.0 / (1.0 + jnp.exp(-jnp.sum(kept, axis=1, keepdims=True)))
-
-
-def finish(ctx, mix_ref, x_ref, x_at, columns_ref, pick_ref, hid_out, rou_out, gate_out):
+def device_index():
+    return lax.axis_index("row") * lax.axis_size("col") + lax.axis_index("col")
+
+
+def own_columns(columns):
+    down = lax.broadcasted_iota(jnp.int32, (256, 256), 0)
+    across = lax.broadcasted_iota(jnp.int32, (256, 256), 1)
+    pick = jnp.where(down == 2 * device_index() + (across >> 7), 1.0, 0.0).astype(BF)
+    return dot(columns, pick).astype(BF)
+
+
+def finish(ctx, mix_ref, x_ref, x_at, hid_out, rou_out):
     for r in range(0, LOOK, 128):
         mixed = dot(ctx[r : r + 128, :], mix_ref[...])
         for s in range(r, r + 128, 32):
             hidden = (x_ref[x_at + s : x_at + s + 32, :].astype(F32) + mixed[s - r : s - r + 32, :]).astype(BF)
             hid_out[s : s + 32, :] = hidden
             rou_out[s : s + 32, :] = norm_rows(hidden.astype(F32))
-        gate_out[r : r + 128, :] = gates(rou_out[r : r + 128, :], columns_ref[...], pick_ref[x_at + r : x_at + r + 128, :])
+
+
+def dispatch(flat, at, routed):
+    place = lax.broadcasted_iota(jnp.int32, (256, LOOK), 0) + at
+    return dot(jnp.where(place == flat, 1.0, 0.0).astype(BF), routed[...]).astype(BF)
+
+
+def wait_last(copies):
+    def step(i, carry):
+        for copy in copies:
+            copy.wait()
+        return carry
+
+    lax.fori_loop(0, jnp.minimum(device_index(), 0) + 1, step, 0)
 
 
 def first_kernel(
-    scale_hbm, x_hbm, w_hbm, mix_hbm, columns_hbm, row_hbm,
-    q_out, acc_out, hid_out, rou_out, gate_out, flat_out, wide_out, pick_out, x_ref, kv_out, mix_ref, columns_ref,
-    normed, wq, q_s, k_s, v_s, ctx, row_ref, scale_ref, sems,
+    scale_hbm, x_hbm, w_hbm, mix_hbm, columns_hbm, row_hbm, entry_hbm, exits_hbm,
+    q_out, acc_out, hid_out, buf_out, flat_out, wide_out, x_ref, kv_out, mix_ref, columns_out, entry_out, exit_out,
+    normed, wq, q_s, k_s, v_s, ctx, routed, columns_ref, row_ref, scale_ref, sems, far_sems,
 ):
     fetch = pltpu.make_async_copy(x_hbm, x_ref, sems.at[0])
     copies = [
@@ -157,7 +173,14 @@
     norm_into(x_ref, normed, T)
     for copy in copies:
         copy.wait()
-    places(row_ref, flat_out, wide_out, pick_out)
+    later = [
+        pltpu.make_async_copy(entry_hbm, entry_out, far_sems.at[0]),
+        pltpu.make_async_copy(exits_hbm.at[0], exit_out, far_sems.at[1]),
+    ]
+    for copy in later:
+        copy.start()
+    places(row_ref, flat_out, wide_out)
+    columns_out[...] = own_columns(columns_ref[...])
     blocks = head_blocks()
     for g in range(3):
         c = slice(g * 256, g * 256 + 256)
@@ -185,13 +208,18 @@
             high += dot(own_weights(dot_t(q1, k1), ahead), v1)
         acc_out[:, pair * 256 : pair * 256 + 256] = low
         ctx[:, c] = (high[:, :LANES] / high[:, LANES:]).astype(BF)
-    finish(ctx, mix_ref, x_ref, LOOK, columns_ref, pick_out, hid_out, rou_out, gate_out)
+    finish(ctx, mix_ref, x_ref, LOOK, hid_out, routed)
+    for s in range(0, SLOTS, 256):
+        buf_out[s : s + 256, :] = dispatch(flat_out[:, LOOK:], s, routed)
+    wait_last(later)
 
 
 def second_kernel(
-    valid_ref, halo_ref, kv_ref, mix_ref, x_ref, columns_ref, q_ref, acc_ref, rou_ref, row_ref, pick_ref,
-    buf_out, hid_out, gate_out, normed, k_s, v_s, ctx, routed,
+    halo_ref, kv_ref, mix_ref, x_ref, q_ref, acc_ref, buf_ref, flat_ref, exits_hbm,
+    buf_out, hid_out, exit_out, normed, k_s, v_s, ctx, routed, far_sem,
 ):
+    later = pltpu.make_async_copy(exits_hbm.at[1], exit_out, far_sem)
+    later.start()
     for r in range(0, LOOK, 32):
         normed[r : r + 32, :] = norm_rows(halo_ref[r : r + 32, :].astype(F32))
     blocks = head_blocks()
@@ -200,7 +228,7 @@
         k_s[:, c] = head_norm(dot(normed[...], kv_ref[:, c]), blocks).astype(BF)
         v_s[:, c] = dot(normed[...], kv_ref[:, D + g * 256 : D + g * 256 + 256]).astype(BF)
     behind, _ = triangles()
-    ones = jnp.full((LOOK, LANES), valid_ref[0].astype(F32)).astype(BF)
+    ones = jnp.full((LOOK, LANES), jnp.minimum(device_index(), 1).astype(F32)).astype(BF)
     for pair in range(PAIRS):
         c = slice(pair * LANES, pair * LANES + LANES)
         low = acc_ref[:, pair * 256 : pair * 256 + 256]
@@ -208,50 +236,48 @@
             q0 = q_ref[:, c] * half_lanes(half)
             low += dot(behind_weights(dot_t(q0, k_s[:, c]), behind), payload(v_s[:, c] * ones, half, ones))
         ctx[:, c] = (low[:, :LANES] / low[:, LANES:]).astype(BF)
-    finish(ctx, mix_ref, x_ref, 0, columns_ref, pick_ref, hid_out, routed, gate_out)
+    finish(ctx, mix_ref, x_ref, 0, hid_out, routed)
     for s in range(0, SLOTS, 256):
-        place = lax.broadcasted_iota(jnp.int32, (256, T), 0) + s
-        pick = jnp.where(place == row_ref[...], 1.0, 0.0).astype(BF)
-        rows = dot(pick[:, :LOOK], routed[...]) + dot(pick[:, LOOK:], rou_ref[...])
-        buf_out[s // 2 : s // 2 + 128] = rows.astype(BF).reshape(128, 2, D)
-
-
-def take_rows(expert):
-    down = lax.broadcasted_iota(jnp.int32, (128, 256), 0)
-    across = lax.broadcasted_iota(jnp.int32, (128, 256), 1)
-    return jnp.where(across == 2 * down + expert, 1.0, 0.0).astype(BF)
-
-
-def put_rows(expert):
-    down = lax.broadcasted_iota(jnp.int32, (256, 128), 0)
-    across = lax.broadcasted_iota(jnp.int32, (256, 128), 1)
-    return jnp.where(down == 2 * across + expert, 1.0, 0.0).astype(BF)
-
-
-def expert_kernel(in_ref, first_ref, second_ref, out_ref, rows, hidden, done):
-    arrived = in_ref[...].reshape(SLOTS, D)
+        rows = dispatch(flat_ref[:, :LOOK], s, routed) + buf_ref[s : s + 256, :]
+        buf_out[s // 2 : s // 2 + 128] = rows.reshape(128, 2, D)
+    wait_last([later])
+
+
+def by_expert(back):
+    down = lax.broadcasted_iota(jnp.int32, (256, 256), 0)
+    across = lax.broadcasted_iota(jnp.int32, (256, 256), 1)
+    if back:
+        down, across = across, down
+    return jnp.where(across == 2 * (down & 127) + (down >> 7), 1.0, 0.0).astype(BF)
+
+
+def expert_kernel(in_ref, columns_ref, first_ref, exit0_ref, exit1_ref, out_ref, rows, hidden, done):
+    order = by_expert(False)
+    for b in range(3):
+        both = dot(order, in_ref[b * 128 : b * 128 + 128].reshape(256, D)).astype(BF)
+        rows[0, b * 128 : b * 128 + 128, :] = both[:128]
+        rows[1, b * 128 : b * 128 + 128, :] = both[128:]
     for e in range(2):
-        pick = take_rows(e)
-        for b in range(3):
-            rows[e, b * 128 : b * 128 + 128, :] = dot(pick, arrived[b * 256 : b * 256 + 256, :]).astype(BF)
-    for e in range(2):
+        logit = dot(rows[e], columns_ref[:, e * LANES : e * LANES + LANES])
+        gate = jnp.concatenate([1.0 / (1.0 + jnp.exp(-logit))] * 2, axis=1)
         for s in range(0, FF, 768):
             hidden[:, s : s + 768] = jnp.maximum(dot(rows[e], first_ref[e, :, s : s + 768]), 0.0).astype(BF)
-        done[e] = dot(hidden[...], second_ref[e]).astype(BF)
+        for s in range(0, D, 256):
+            done[e, :, s : s + 256] = (gate * dot(hidden[...], (exit0_ref, exit1_ref)[e][:, s : s + 256])).astype(BF)
+    order = by_expert(True)
     for b in range(3):
         r = slice(b * 128, b * 128 + 128)
-        mixed = dot(put_rows(0), done[0, r, :]) + dot(put_rows(1), done[1, r, :])
-        out_ref[r] = mixed.astype(BF).reshape(128, 2, D)
-
-
-def last_kernel(back_ref, hid0_ref, hid1_ref, gate0_ref, gate1_ref, wide_ref, out_ref):
+        both = jnp.concatenate([done[0, r, :], done[1, r, :]], axis=0)
+        out_ref[r] = dot(order, both).astype(BF).reshape(128, 2, D)
+
+
+def last_kernel(back_ref, hid0_ref, hid1_ref, wide_ref, out_ref):
     back = back_ref[...].reshape(SLOTS, D)
-    for r, hid_ref, gate_ref in ((0, hid0_ref, gate0_ref), (LOOK, hid1_ref, gate1_ref)):
+    for r, hid_ref in ((0, hid0_ref), (LOOK, hid1_ref)):
         across = lax.broadcasted_iota(jnp.int32, (LOOK, SLOTS), 1)
         place = jnp.concatenate([wide_ref[r : r + LOOK, :]] * 6, axis=1)
         pick = jnp.where(across == place, 1.0, 0.0).astype(BF)
-        picked = dot(pick, back)
-        out_ref[r : r + LOOK, :] = (hid_ref[...].astype(F32) + gate_ref[...] * picked).astype(BF)
+        out_ref[r : r + LOOK, :] = (hid_ref[...].astype(F32) + dot(pick, back)).astype(BF)
 
 
 def params(limit):
@@ -270,71 +296,96 @@
     return pltpu.with_memory_space_constraint(value, pltpu.HBM)
 
 
-def shards(x, triple, mixing, scaling, columns, pick, entry, exits):
-    steps = [(i, i + 1) for i in range(127)]
-    halo = lax.ppermute(x[T - LOOK :], AXES, steps)
-    row = pick.reshape(1, T)
-    vmem = pl.BlockSpec(memory_space=pltpu.VMEM)
-    smem = pl.BlockSpec(memory_space=pltpu.SMEM)
-    hbm = pl.BlockSpec(memory_space=pltpu.HBM)
-    q0, acc0, hid1, rou1, gate1, flat, wide, chosen, x_near, kv, mix_near, columns_near = pl.pallas_call(
+VM = pl.BlockSpec(memory_space=pltpu.VMEM)
+HB = pl.BlockSpec(memory_space=pltpu.HBM)
+
+
+def call_first(scaling, x, triple, mixing, columns, row, entry, exits):
+    return pl.pallas_call(
         first_kernel,
         out_shape=(
             shape(LOOK, D),
             shape(LOOK, 2 * D, dtype=F32),
             shape(LOOK, D),
-            shape(LOOK, D),
-            shape(LOOK, 1, dtype=F32),
+            shape(SLOTS, D),
             shape(1, T, dtype=jnp.int32),
-            shape(T, LANES, dtype=jnp.int32),
             shape(T, LANES, dtype=jnp.int32),
             shape(T, D),
             shape(D, 2 * D),
             shape(D, D),
             shape(D, 256),
+            shape(2, D, FF),
+            shape(FF, D),
         ),
-        in_specs=[hbm] * 6,
-        out_specs=(vmem,) * 12,
+        in_specs=[HB] * 8,
+        out_specs=(VM,) * 12,
         scratch_shapes=[pltpu.VMEM((T, D), BF), pltpu.VMEM((D, D), BF)]
         + [pltpu.VMEM((T, D), BF)] * 3
         + [
             pltpu.VMEM((LOOK, D), BF),
+            pltpu.VMEM((LOOK, D), BF),
+            pltpu.VMEM((D, 256), BF),
             pltpu.VMEM((1, T), jnp.int32),
             pltpu.SMEM((HEADS,), F32),
             pltpu.SemaphoreType.DMA((7,)),
+            pltpu.SemaphoreType.DMA((2,)),
         ],
         compiler_params=params(16),
         cost_estimate=cost(4 * 10**9, 8 * MB),
         name="first",
-    )(*(far(a) for a in (scaling, x, triple, mixing, columns, row)))
-    valid = jnp.minimum(lax.axis_index(AXES), 1).astype(jnp.int32).reshape(1)
-    buf, hid0, gate0 = pl.pallas_call(
+    )(*(far(a) for a in (scaling, x, triple, mixing, columns, row, entry, exits)))
+
+
+def call_second(halo, kv, mixing, x, q0, acc0, buf1, flat, exits):
+    return pl.pallas_call(
         second_kernel,
-        out_shape=(shape(SLOTS // 2, 2, D), shape(LOOK, D), shape(LOOK, 1, dtype=F32)),
-        in_specs=[smem] + [vmem] * 10,
-        out_specs=(vmem,) * 3,
-        scratch_shapes=[pltpu.VMEM((LOOK, D), BF)] * 5,
+        out_shape=(shape(SLOTS // 2, 2, D), shape(LOOK, D), shape(FF, D)),
+        in_specs=[VM] * 8 + [HB],
+        out_specs=(VM,) * 3,
+        scratch_shapes=[pltpu.VMEM((LOOK, D), BF)] * 5 + [pltpu.SemaphoreType.DMA],
         compiler_params=params(16),
         cost_estimate=cost(2 * 10**9, 8 * MB),
         name="second",
-    )(valid, halo, kv, mix_near, x_near, columns_near, q0, acc0, rou1, flat, chosen)
-    arrived = lax.all_to_all(buf.reshape(128, CAP, 2, D), AXES, split_axis=0, concat_axis=0, tiled=True)
-    out = pl.pallas_call(
+    )(halo, kv, mixing, x, q0, acc0, buf1, flat, far(exits))
+
+
+def call_experts(arrived, columns, entry, exit0, exit1):
+    return pl.pallas_call(
         expert_kernel,
         out_shape=shape(SLOTS // 2, 2, D),
-        scratch_shapes=[pltpu.VMEM((2, SLOTS // 2, D), BF), pltpu.VMEM((SLOTS // 2, FF), BF), pltpu.VMEM((2, SLOTS // 2, D), BF)],
+        scratch_shapes=[
+            pltpu.VMEM((2, SLOTS // 2, D), BF),
+            pltpu.VMEM((SLOTS // 2, FF), BF),
+            pltpu.VMEM((2, SLOTS // 2, D), BF),
+        ],
         compiler_params=params(14),
         cost_estimate=cost(7 * 10**9, 20 * MB),
         name="experts",
-    )(arrived.reshape(SLOTS // 2, 2, D), entry, exits)
-    back = lax.all_to_all(out.reshape(128, CAP, 2, D), AXES, split_axis=0, concat_axis=0, tiled=True)
+    )(arrived, columns, entry, exit0, exit1)
+
+
+def call_last(back, hid0, hid1, wide):
     return pl.pallas_call(
         last_kernel,
         out_shape=shape(T, D),
         compiler_params=params(16),
         cost_estimate=cost(6 * 10**8, 3 * MB),
         name="last",
-    )(back.reshape(SLOTS // 2, 2, D), hid0, hid1, gate0, gate1, wide)
+    )(back, hid0, hid1, wide)
+
+
+def exchange(rows):
+    rows = rows.reshape(128, CAP, 2, D)
+    return lax.all_to_all(rows, AXES, split_axis=0, concat_axis=0, tiled=True).reshape(SLOTS // 2, 2, D)
+
+
+def shards(x, triple, mixing, scaling, columns, pick, entry, exits):
+    halo = lax.ppermute(x[T - LOOK :], AXES, [(i, i + 1) for i in range(127)])
+    first = call_first(scaling, x, triple, mixing, columns, pick.reshape(1, T), entry, exits)
+    q0, acc0, hid1, buf1, flat, wide, x_near, kv, mix_near, columns_near, entry_near, exit0 = first
+    buf, hid0, exit1 = call_second(halo, kv, mix_near, x_near, q0, acc0, buf1, flat, exits)
+    back = exchange(call_experts(exchange(buf), columns_near, entry_near, exit0, exit1))
+    return call_last(back, hid0, hid1, wide)
 
 
 def solution(mesh):

time: 87.4 us -> 89.6 us (1.025)
  Pallas kernels: 26.8 us -> 29.2 us
  waiting for transfers between devices: 1.67 us -> 0.01 us
  blocking collectives: 53.6 us -> 55.2 us
    pallas_call x4, Pallas kernels: 26.8 us -> 29.2 us  [the longest x1 13.1 us: call_first(): pl.pallas_call(first_kernel, out_shape=(shape(LOOK, D), shape(LOOK, 2 * D...]
    ppermute x1, waiting for transfers between devices: 1.67 us -> 0.01 us  [shards(): halo = lax.ppermute(x[T - LOOK:], AXES, [(i, i + 1) for i in range(127)])]
    all_to_all x2, blocking collectives: 53.6 us -> 55.2 us  [exchange(): lax.all_to_all(rows, AXES, split_axis=0, concat_axis=0, tiled=True)]
  transfers between devices with their start and end apart: 1 -> 1, of which waited for: 1 -> 0; matrix products, arithmetic and copies ran while one was open for 0% -> 0% of each run, Pallas kernels for 13% -> 15%
where the time goes in v3:
time: 89.6 us; the launch traced here: 89.4 us
  blocking collectives  55.2 us (62%)
  Pallas kernels  29.2 us (33%)
  starting transfers between devices  3.95 us (4%)
  local copies, waits for them, and re-layouts  1.02 us (1%)
    all_to_all x2, blocking collectives, exchange(): lax.all_to_all(rows, AXES, split_axis=0, concat_axis=0, tiled=True)  55.2 us
    pallas_call x1, Pallas kernels, call_first(): pl.pallas_call(first_kernel, out_shape=(shape(LOOK, D), shape(LOOK, 2 * D...  13.1 us
    pallas_call x1, Pallas kernels, call_experts(): pl.pallas_call(expert_kernel, out_shape=shape(SLOTS // 2, 2, D), scratch_...  9.29 us
    pallas_call x1, Pallas kernels, call_second(): pl.pallas_call(second_kernel, out_shape=(shape(SLOTS // 2, 2, D), shape(L...  5.08 us
    ppermute x1, starting transfers between devices, shards(): halo = lax.ppermute(x[T - LOOK:], AXES, [(i, i + 1) for i in range(127)])  3.95 us
  transfers between devices with their start and end apart: 1, of which 0 were waited for; matrix products, arithmetic and copies ran while one was open for 0% of the time, Pallas kernels for 15%

profile of v3, /device:TPU:1, one launch (start us, length us, event | category | flops | bytes accessed | tf_op | source)
XLA Modules:
  0.0 89.4 jit_solution(14953390498470604263)
XLA Ops:
  0.0 1.0 %slice.3 = bf16[256,768]{1,0:T(8,128)(2,1)S(1)} slice(bf16[512,768]{1,0:T(8,128)(2,1)} %x_hbm.1), slice={[256:512], [0:768]} | slice | bytes 786432 | tf_op jit(solution)/shard_map/slice | solution.py:383
  1.0 3.9 %collective-permute-start = (bf16[256,768]{1,0:T(8,128)(2,1)S(1)}, bf16[256,768]{1,0:T(8,128)(2,1)S(1)}, u32[]{:S(2)}, u32[]{:S(2)}) collective-permute-start(bf16[256,768]{1,0:T(8,128)(2,1)S(1)} %slice.3), channel_id=1, source_target_pairs={{0,1},{1,2},{2,3},{3,4},{4,5},{5,6},{6,7},{7,8},{8,9},{9,10},{10,1... | collective-permute-start | bytes 1179656 | tf_op jit(solution)/shard_map/ppermute | solution.py:383
  5.0 13.1 %first.1 = (bf16[256,768]{1,0:T(8,128)(2,1)S(1)}, f32[256,1536]{1,0:T(8,128)S(1)}, bf16[256,768]{1,0:T(8,128)(2,1)S(1)}, bf16[768,768]{1,0:T(8,128)(2,1)S(1)}, s...) custom-call(f32[12]{0:T(128)} %scale_hbm.1, ...), custom_call_target="tpu_custom_call" | custom-call | flops 4000000000 | bytes 8388608 | tf_op jit(solution)/shard_map/first/pallas_call | solution.py:304
  18.1 0.0 collective-permute-done.halo_ref
  18.1 5.1 %second.1 = (bf16[384,2,768]{2,1,0:T(2,128)(2,1)S(1)}, bf16[256,768]{1,0:T(8,128)(2,1)S(1)}, bf16[3072,768]{1,0:T(8,128)(2,1)S(1)}) custom-call(bf16[256,768]{1,0:T(8,128)(2,1)S(1)} %collective-permute-done.halo_ref, bf16[768,1536]{1,0:T(8,128)(2,1)S(1)} %get-tuple-element.20.kv_ref, bf16[768,768]{1,0:T(8,128)(2,1)S(1)} %get-tuple-element.21.mix_ref, ...), custom_call_target="tpu_custom_call" | custom-call | flops 2000000000 | bytes 8388608 | tf_op jit(solution)/shard_map/second/pallas_call | solution.py:340
  23.2 30.7 %all_to_all.10 = bf16[128,3,2,768]{3,2,1,0:T(2,128)(2,1)S(1)} all-to-all(bf16[128,3,2,768]{3,2,1,0:T(2,128)(2,1)S(1)} %bitcast.6), channel_id=1, replica_groups=mesh['row'=8,'col'=16] {'row','col'}, dimensions={0} | all-to-all | bytes 2359296 | tf_op jit(solution)/shard_map/all_to_all | solution.py:379
  53.8 9.3 %experts.1 = bf16[384,2,768]{2,1,0:T(2,128)(2,1)S(1)} custom-call(bf16[384,2,768]{2,1,0:T(2,128)(2,1)S(1)} %bitcast.7, bf16[768,256]{1,0:T(8,128)(2,1)S(1)} %get-tuple-element.28.columns_ref, bf16[2,768,3072]{2,1,0:T(8,128)(2,1)S(1)} %get-tuple-element.29.first_ref, bf16[3072,768]{1,0:T(8,128)(2,1)S(1)} %get-tuple-element.30.exit0_ref, ...), custom_call_target="tpu_custom_call" | custom-call | flops 7000000000 | bytes 20971520 | tf_op jit(solution)/shard_map/experts/pallas_call | solution.py:353
  63.1 24.5 %all_to_all.11 = bf16[128,3,2,768]{3,2,1,0:T(2,128)(2,1)S(1)} all-to-all(bf16[128,3,2,768]{3,2,1,0:T(2,128)(2,1)S(1)} %bitcast.8), channel_id=1, replica_groups=mesh['row'=8,'col'=16] {'row','col'}, dimensions={0} | all-to-all | bytes 2359296 | tf_op jit(solution)/shard_map/all_to_all | solution.py:379
  87.6 1.7 %last.1 = bf16[512,768]{1,0:T(8,128)(2,1)} custom-call(bf16[384,2,768]{2,1,0:T(2,128)(2,1)S(1)} %bitcast.5, bf16[256,768]{1,0:T(8,128)(2,1)S(1)} %get-tuple-element.32.hid0_ref, bf16[256,768]{1,0:T(8,128)(2,1)S(1)} %get-tuple-element.33.hid1_ref, s32[512,128]{1,0:T(8,128)S(1)} %get-tuple-element.34.wide_ref), custom_call_target="tpu_custom_call" | custom-call | flops 600000000 | bytes 3145728 | tf_op jit(solution)/shard_map/last/pallas_call | solution.py:368
Async XLA Ops:
  1.0 17.0 %collective-permute-start = (bf16[256,768]{1,0:T(8,128)(2,1)S(1)}, bf16[256,768]{1,0:T(8,128)(2,1)S(1)}, u32[]{:S(2)}, u32[]{:S(2)}) collective-permute-start(bf16[256,768]{1,0:T(8,128)(2,1)S(1)} %slice.3), channel_id=1, source_target_pairs={{0,1},{1,2},{2,3},{3,4},{4,5},{5,6},{6,7},{7,8},{8,9},{9,10},{10,1... | collective-permute-start | bytes 1179656 | tf_op jit(solution)/shard_map/ppermute | solution.py:383

commit v4 on v3

--- a/solution.py
+++ b/solution.py
@@ -129,11 +129,11 @@
     return dot(columns, pick).astype(BF)
 
 
-def finish(ctx, mix_ref, x_ref, x_at, hid_out, rou_out):
+def finish(ctx, mix_ref, x_ref, hid_out, rou_out):
     for r in range(0, LOOK, 128):
         mixed = dot(ctx[r : r + 128, :], mix_ref[...])
         for s in range(r, r + 128, 32):
-            hidden = (x_ref[x_at + s : x_at + s + 32, :].astype(F32) + mixed[s - r : s - r + 32, :]).astype(BF)
+            hidden = (x_ref[s : s + 32, :].astype(F32) + mixed[s - r : s - r + 32, :]).astype(BF)
             hid_out[s : s + 32, :] = hidden
             rou_out[s : s + 32, :] = norm_rows(hidden.astype(F32))
 
@@ -143,44 +143,55 @@
     return dot(jnp.where(place == flat, 1.0, 0.0).astype(BF), routed[...]).astype(BF)
 
 
-def wait_last(copies):
+def apart(work):
     def step(i, carry):
-        for copy in copies:
-            copy.wait()
+        work()
         return carry
 
     lax.fori_loop(0, jnp.minimum(device_index(), 0) + 1, step, 0)
 
 
+def load_kernel(x_hbm, low_out, high_out, normed_out, sems):
+    high = pltpu.make_async_copy(x_hbm.at[pl.ds(LOOK, LOOK), :], high_out, sems.at[0])
+    low = pltpu.make_async_copy(x_hbm.at[pl.ds(0, LOOK), :], low_out, sems.at[1])
+    high.start()
+    low.start()
+    high.wait()
+    low.wait()
+    for r in range(0, LOOK, 32):
+        normed_out[r : r + 32, :] = norm_rows(high_out[r : r + 32, :].astype(F32))
+
+
 def first_kernel(
-    scale_hbm, x_hbm, w_hbm, mix_hbm, columns_hbm, row_hbm, entry_hbm, exits_hbm,
-    q_out, acc_out, hid_out, buf_out, flat_out, wide_out, x_ref, kv_out, mix_ref, columns_out, entry_out, exit_out,
-    normed, wq, q_s, k_s, v_s, ctx, routed, columns_ref, row_ref, scale_ref, sems, far_sems,
+    low_ref, high_ref, normed_ref, scale_hbm, w_hbm, mix_hbm, columns_hbm, row_hbm,
+    q_out, acc_out, hid_out, buf_out, flat_out, wide_out, kv_out, mix_ref, columns_out,
+    normed, wq, q_s, k_s, v_s, ctx, routed, columns_ref, row_ref, scale_ref, sems,
 ):
-    fetch = pltpu.make_async_copy(x_hbm, x_ref, sems.at[0])
-    copies = [
+    early = [
+        pltpu.make_async_copy(row_hbm, row_ref, sems.at[5]),
+        pltpu.make_async_copy(columns_hbm, columns_ref, sems.at[3]),
+    ]
+    dense = [
         pltpu.make_async_copy(w_hbm.at[:, pl.ds(0, D)], wq, sems.at[1]),
         pltpu.make_async_copy(w_hbm.at[:, pl.ds(D, 2 * D)], kv_out, sems.at[2]),
-        pltpu.make_async_copy(columns_hbm, columns_ref, sems.at[3]),
-        pltpu.make_async_copy(mix_hbm, mix_ref, sems.at[4]),
-        pltpu.make_async_copy(row_hbm, row_ref, sems.at[5]),
         pltpu.make_async_copy(scale_hbm, scale_ref, sems.at[6]),
     ]
-    fetch.start()
-    for copy in copies:
+    mix = [pltpu.make_async_copy(mix_hbm, mix_ref, sems.at[4])]
+    for copy in early + dense + mix:
         copy.start()
-    fetch.wait()
-    norm_into(x_ref, normed, T)
-    for copy in copies:
+    for copy in early:
         copy.wait()
-    later = [
-        pltpu.make_async_copy(entry_hbm, entry_out, far_sems.at[0]),
-        pltpu.make_async_copy(exits_hbm.at[0], exit_out, far_sems.at[1]),
-    ]
-    for copy in later:
-        copy.start()
-    places(row_ref, flat_out, wide_out)
-    columns_out[...] = own_columns(columns_ref[...])
+
+    def prepare():
+        for r in range(0, LOOK, 32):
+            normed[r : r + 32, :] = norm_rows(low_ref[r : r + 32, :].astype(F32))
+        normed[LOOK:, :] = normed_ref[...]
+        places(row_ref, flat_out, wide_out)
+        columns_out[...] = own_columns(columns_ref[...])
+
+    apart(prepare)
+    for copy in dense:
+        copy.wait()
     blocks = head_blocks()
     for g in range(3):
         c = slice(g * 256, g * 256 + 256)
@@ -208,25 +219,21 @@
             high += dot(own_weights(dot_t(q1, k1), ahead), v1)
         acc_out[:, pair * 256 : pair * 256 + 256] = low
         ctx[:, c] = (high[:, :LANES] / high[:, LANES:]).astype(BF)
-    finish(ctx, mix_ref, x_ref, LOOK, hid_out, routed)
+    apart(mix[0].wait)
+    finish(ctx, mix_ref, high_ref, hid_out, routed)
     for s in range(0, SLOTS, 256):
         buf_out[s : s + 256, :] = dispatch(flat_out[:, LOOK:], s, routed)
-    wait_last(later)
 
 
 def second_kernel(
-    halo_ref, kv_ref, mix_ref, x_ref, q_ref, acc_ref, buf_ref, flat_ref, exits_hbm,
-    buf_out, hid_out, exit_out, normed, k_s, v_s, ctx, routed, far_sem,
+    halo_ref, kv_ref, mix_ref, x_ref, q_ref, acc_ref, buf_ref, flat_ref,
+    buf_out, hid_out, k_s, v_s, ctx, routed,
 ):
-    later = pltpu.make_async_copy(exits_hbm.at[1], exit_out, far_sem)
-    later.start()
-    for r in range(0, LOOK, 32):
-        normed[r : r + 32, :] = norm_rows(halo_ref[r : r + 32, :].astype(F32))
     blocks = head_blocks()
     for g in range(3):
         c = slice(g * 256, g * 256 + 256)
-        k_s[:, c] = head_norm(dot(normed[...], kv_ref[:, c]), blocks).astype(BF)
-        v_s[:, c] = dot(normed[...], kv_ref[:, D + g * 256 : D + g * 256 + 256]).astype(BF)
+        k_s[:, c] = head_norm(dot(halo_ref[...], kv_ref[:, c]), blocks).astype(BF)
+        v_s[:, c] = dot(halo_ref[...], kv_ref[:, D + g * 256 : D + g * 256 + 256]).astype(BF)
     behind, _ = triangles()
     ones = jnp.full((LOOK, LANES), jnp.minimum(device_index(), 1).astype(F32)).astype(BF)
     for pair in range(PAIRS):
@@ -236,11 +243,10 @@
             q0 = q_ref[:, c] * half_lanes(half)
             low += dot(behind_weights(dot_t(q0, k_s[:, c]), behind), payload(v_s[:, c] * ones, half, ones))
         ctx[:, c] = (low[:, :LANES] / low[:, LANES:]).astype(BF)
-    finish(ctx, mix_ref, x_ref, 0, hid_out, routed)
+    finish(ctx, mix_ref, x_ref, hid_out, routed)
     for s in range(0, SLOTS, 256):
         rows = dispatch(flat_ref[:, :LOOK], s, routed) + buf_ref[s : s + 256, :]
         buf_out[s // 2 : s // 2 + 128] = rows.reshape(128, 2, D)
-    wait_last([later])
 
 
 def by_expert(back):
@@ -251,7 +257,7 @@
     return jnp.where(across == 2 * (down & 127) + (down >> 7), 1.0, 0.0).astype(BF)
 
 
-def expert_kernel(in_ref, columns_ref, first_ref, exit0_ref, exit1_ref, out_ref, rows, hidden, done):
+def expert_kernel(in_ref, columns_ref, first_ref, second_ref, out_ref, rows, hidden, done):
     order = by_expert(False)
     for b in range(3):
         both = dot(order, in_ref[b * 128 : b * 128 + 128].reshape(256, D)).astype(BF)
@@ -263,7 +269,7 @@
         for s in range(0, FF, 768):
             hidden[:, s : s + 768] = jnp.maximum(dot(rows[e], first_ref[e, :, s : s + 768]), 0.0).astype(BF)
         for s in range(0, D, 256):
-            done[e, :, s : s + 256] = (gate * dot(hidden[...], (exit0_ref, exit1_ref)[e][:, s : s + 256])).astype(BF)
+            done[e, :, s : s + 256] = (gate * dot(hidden[...], second_ref[e, :, s : s + 256])).astype(BF)
     order = by_expert(True)
     for b in range(3):
         r = slice(b * 128, b * 128 + 128)
@@ -271,13 +277,21 @@
         out_ref[r] = dot(order, both).astype(BF).reshape(128, 2, D)
 
 
-def last_kernel(back_ref, hid0_ref, hid1_ref, wide_ref, out_ref):
+def last_kernel(back_ref, hid0_ref, hid1_ref, wide_ref, out_hbm, out, sems):
     back = back_ref[...].reshape(SLOTS, D)
-    for r, hid_ref in ((0, hid0_ref), (LOOK, hid1_ref)):
-        across = lax.broadcasted_iota(jnp.int32, (LOOK, SLOTS), 1)
-        place = jnp.concatenate([wide_ref[r : r + LOOK, :]] * 6, axis=1)
+    copies = []
+    for i in range(4):
+        r = slice(i * 128, i * 128 + 128)
+        hid_ref = (hid0_ref, hid1_ref)[i // 2]
+        across = lax.broadcasted_iota(jnp.int32, (128, SLOTS), 1)
+        place = jnp.concatenate([wide_ref[r, :]] * 6, axis=1)
         pick = jnp.where(across == place, 1.0, 0.0).astype(BF)
-        out_ref[r : r + LOOK, :] = (hid_ref[...].astype(F32) + dot(pick, back)).astype(BF)
+        hidden = hid_ref[i % 2 * 128 : i % 2 * 128 + 128, :].astype(F32)
+        out[r, :] = (hidden + dot(pick, back)).astype(BF)
+        copies.append(pltpu.make_async_copy(out.at[r, :], out_hbm.at[r, :], sems.at[i]))
+        copies[-1].start()
+    for copy in copies:
+        copy.wait()
 
 
 def params(limit):
@@ -300,7 +314,20 @@
 HB = pl.BlockSpec(memory_space=pltpu.HBM)
 
 
-def call_first(scaling, x, triple, mixing, columns, row, entry, exits):
+def call_load(x):
+    return pl.pallas_call(
+        load_kernel,
+        out_shape=(shape(LOOK, D),) * 3,
+        in_specs=[HB],
+        out_specs=(VM,) * 3,
+        scratch_shapes=[pltpu.SemaphoreType.DMA((2,))],
+        compiler_params=params(8),
+        cost_estimate=cost(10**6, MB),
+        name="load",
+    )(far(x))
+
+
+def call_first(low, high, normed, scaling, triple, mixing, columns, row):
     return pl.pallas_call(
         first_kernel,
         out_shape=(
@@ -310,15 +337,12 @@
             shape(SLOTS, D),
             shape(1, T, dtype=jnp.int32),
             shape(T, LANES, dtype=jnp.int32),
-            shape(T, D),
             shape(D, 2 * D),
             shape(D, D),
             shape(D, 256),
-            shape(2, D, FF),
-            shape(FF, D),
         ),
-        in_specs=[HB] * 8,
-        out_specs=(VM,) * 12,
+        in_specs=[VM] * 3 + [HB] * 5,
+        out_specs=(VM,) * 9,
         scratch_shapes=[pltpu.VMEM((T, D), BF), pltpu.VMEM((D, D), BF)]
         + [pltpu.VMEM((T, D), BF)] * 3
         + [
@@ -328,28 +352,27 @@
             pltpu.VMEM((1, T), jnp.int32),
             pltpu.SMEM((HEADS,), F32),
             pltpu.SemaphoreType.DMA((7,)),
-            pltpu.SemaphoreType.DMA((2,)),
         ],
         compiler_params=params(16),
         cost_estimate=cost(4 * 10**9, 8 * MB),
         name="first",
-    )(*(far(a) for a in (scaling, x, triple, mixing, columns, row, entry, exits)))
-
-
-def call_second(halo, kv, mixing, x, q0, acc0, buf1, flat, exits):
+    )(low, high, normed, *(far(a) for a in (scaling, triple, mixing, columns, row)))
+
+
+def call_second(halo, kv, mixing, x, q0, acc0, buf1, flat):
     return pl.pallas_call(
         second_kernel,
-        out_shape=(shape(SLOTS // 2, 2, D), shape(LOOK, D), shape(FF, D)),
-        in_specs=[VM] * 8 + [HB],
-        out_specs=(VM,) * 3,
-        scratch_shapes=[pltpu.VMEM((LOOK, D), BF)] * 5 + [pltpu.SemaphoreType.DMA],
+        out_shape=(shape(SLOTS // 2, 2, D), shape(LOOK, D)),
+        in_specs=[VM] * 8,
+        out_specs=(VM,) * 2,
+        scratch_shapes=[pltpu.VMEM((LOOK, D), BF)] * 4,
         compiler_params=params(16),
-        cost_estimate=cost(2 * 10**9, 8 * MB),
+        cost_estimate=cost(30 * 10**9, 8 * MB),
         name="second",
-    )(halo, kv, mixing, x, q0, acc0, buf1, flat, far(exits))
-
-
-def call_experts(arrived, columns, entry, exit0, exit1):
+    )(halo, kv, mixing, x, q0, acc0, buf1, flat)
+
+
+def call_experts(arrived, columns, entry, exits):
     return pl.pallas_call(
         expert_kernel,
         out_shape=shape(SLOTS // 2, 2, D),
@@ -361,13 +384,16 @@
         compiler_params=params(14),
         cost_estimate=cost(7 * 10**9, 20 * MB),
         name="experts",
-    )(arrived, columns, entry, exit0, exit1)
+    )(arrived, columns, entry, exits)
 
 
 def call_last(back, hid0, hid1, wide):
     return pl.pallas_call(
         last_kernel,
         out_shape=shape(T, D),
+        in_specs=[VM] * 4,
+        out_specs=HB,
+        scratch_shapes=[pltpu.VMEM((T, D), BF), pltpu.SemaphoreType.DMA((4,))],
         compiler_params=params(16),
         cost_estimate=cost(6 * 10**8, 3 * MB),
         name="last",
@@ -380,11 +406,12 @@
 
 
 def shards(x, triple, mixing, scaling, columns, pick, entry, exits):
-    halo = lax.ppermute(x[T - LOOK :], AXES, [(i, i + 1) for i in range(127)])
-    first = call_first(scaling, x, triple, mixing, columns, pick.reshape(1, T), entry, exits)
-    q0, acc0, hid1, buf1, flat, wide, x_near, kv, mix_near, columns_near, entry_near, exit0 = first
-    buf, hid0, exit1 = call_second(halo, kv, mix_near, x_near, q0, acc0, buf1, flat, exits)
-    back = exchange(call_experts(exchange(buf), columns_near, entry_near, exit0, exit1))
+    low, high, normed = call_load(x)
+    halo = lax.ppermute(normed, AXES, [(i, i + 1) for i in range(127)])
+    first = call_first(low, high, normed, scaling, triple, mixing, columns, pick.reshape(1, T))
+    q0, acc0, hid1, buf1, flat, wide, kv, mix_near, columns_near = first
+    buf, hid0 = call_second(halo, kv, mix_near, low, q0, acc0, buf1, flat)
+    back = exchange(call_experts(exchange(buf), columns_near, entry, exits))
     return call_last(back, hid0, hid1, wide)
 
 

time: 89.6 us -> 85.2 us (0.951)
  Pallas kernels: 29.2 us -> 25.5 us
  waiting for transfers between devices: 0.01 us -> 2.98 us
  blocking collectives: 55.2 us -> 52.3 us
  local copies, waits for them, and re-layouts: 1.02 us -> 0.03 us
    pallas_call x1, Pallas kernels: 13.1 us -> 10 us  [call_first(): pl.pallas_call(first_kernel, out_shape=(shape(LOOK, D), shape(LOOK, 2 * D...]
    ppermute x1, waiting for transfers between devices: 0.01 us -> 2.98 us  [shards(): halo = lax.ppermute(normed, AXES, [(i, i + 1) for i in range(127)])]
    all_to_all x2, blocking collectives: 55.2 us -> 52.3 us  [exchange(): lax.all_to_all(rows, AXES, split_axis=0, concat_axis=0, tiled=True)]
    pallas_call x1, Pallas kernels: 5.08 us -> 3.28 us  [call_second(): pl.pallas_call(second_kernel, out_shape=(shape(SLOTS // 2, 2, D), shape(L...]
    pallas_call x1 -> x2, Pallas kernels: 1.74 us -> 2.99 us  [the longest x1 1.57 us: call_last(): pl.pallas_call(last_kernel, out_shape=shape(T, D), in_specs=[VM] * 4, out...]
    slice x1 -> x0, local copies, waits for them, and re-layouts: 1.02 us -> none  [shards(): halo = lax.ppermute(x[T - LOOK:], AXES, [(i, i + 1) for i in range(127)])]
  transfers between devices with their start and end apart: 1 -> 1, of which waited for: 0 -> 1; matrix products, arithmetic and copies ran while one was open for 0% -> 0% of each run, Pallas kernels for 15% -> 12%
where the time goes in v4:
time: 85.2 us; the launch traced here: 85 us
  blocking collectives  52.3 us (61%)
  Pallas kernels  25.5 us (30%)
  starting transfers between devices  3.95 us (5%)
  waiting for transfers between devices  2.98 us (3%)
    all_to_all x2, blocking collectives, exchange(): lax.all_to_all(rows, AXES, split_axis=0, concat_axis=0, tiled=True)  52.3 us
    pallas_call x1, Pallas kernels, call_first(): pl.pallas_call(first_kernel, out_shape=(shape(LOOK, D), shape(LOOK, 2 * D...  10 us
    pallas_call x1, Pallas kernels, call_experts(): pl.pallas_call(expert_kernel, out_shape=shape(SLOTS // 2, 2, D), scratch_...  9.24 us
    ppermute x1, starting transfers between devices, shards(): halo = lax.ppermute(normed, AXES, [(i, i + 1) for i in range(127)])  3.95 us
    pallas_call x1, Pallas kernels, call_second(): pl.pallas_call(second_kernel, out_shape=(shape(SLOTS // 2, 2, D), shape(L...  3.28 us
    ppermute x1, waiting for transfers between devices, shards(): halo = lax.ppermute(normed, AXES, [(i, i + 1) for i in range(127)])  2.98 us
  transfers between devices with their start and end apart: 1, of which 1 were waited for; matrix products, arithmetic and copies ran while one was open for 0% of the time, Pallas kernels for 12%

profile of v4, /device:TPU:1, one launch (start us, length us, event | category | flops | bytes accessed | tf_op | source)
XLA Modules:
  0.0 85.0 jit_solution(18137222343093492762)
XLA Ops:
  0.0 1.4 %load.1 = (bf16[256,768]{1,0:T(8,128)(2,1)S(1)}, bf16[256,768]{1,0:T(8,128)(2,1)S(1)}, bf16[256,768]{1,0:T(8,128)(2,1)S(1)}) custom-call(bf16[512,768]{1,0:T(8,128)(2,1)} %x_hbm.1), custom_call_target="tpu_custom_call" | custom-call | flops 1000000 | bytes 1048576 | tf_op jit(solution)/shard_map/load/pallas_call | solution.py:318
  1.4 3.9 %collective-permute-start = (bf16[256,768]{1,0:T(8,128)(2,1)S(1)}, bf16[256,768]{1,0:T(8,128)(2,1)S(1)}, u32[]{:S(2)}, u32[]{:S(2)}) collective-permute-start(bf16[256,768]{1,0:T(8,128)(2,1)S(1)} %get-tuple-element.19.normed_ref), channel_id=1, source_target_pairs={{0,1},{1,2},{2,3},{3,4},{4,5},{5,6},{6,7},{7,8},{8,9},{9,10},{10,1... | collective-permute-start | bytes 1179656 | tf_op jit(solution)/shard_map/ppermute | solution.py:410
  5.4 0.0 slice-start
  5.4 0.0 slice-start.3
  5.4 10.0 %first.1 = (bf16[256,768]{1,0:T(8,128)(2,1)S(1)}, f32[256,1536]{1,0:T(8,128)S(1)}, bf16[256,768]{1,0:T(8,128)(2,1)S(1)}, bf16[768,768]{1,0:T(8,128)(2,1)S(1)}, s...) custom-call(bf16[256,768]{1,0:T(8,128)(2,1)S(1)} %get-tuple-element., ...), custom_call_target="tpu_custom_call" | custom-call | flops 4000000000 | bytes 8388608 | tf_op jit(solution)/shard_map/first/pallas_call | solution.py:331
  15.4 3.0 %collective-permute-done.halo_ref = bf16[256,768]{1,0:T(8,128)(2,1)S(1)} collective-permute-done((bf16[256,768]{1,0:T(8,128)(2,1)S(1)}, bf16[256,768]{1,0:T(8,128)(2,1)S(1)}, u32[]{:S(2)}, u32[]{:S(2)}) %collective-permute-start) | collective-permute-done | bytes 393248 | tf_op jit(solution)/shard_map/ppermute | solution.py:410
  18.4 0.0 slice-start.1
  18.4 0.0 slice-start.2
  18.4 0.0 slice-start.4
  18.4 0.0 slice-start.5
  18.4 3.3 %second.1 = (bf16[384,2,768]{2,1,0:T(2,128)(2,1)S(1)}, bf16[256,768]{1,0:T(8,128)(2,1)S(1)}) custom-call(bf16[256,768]{1,0:T(8,128)(2,1)S(1)} %collective-permute-done.halo_ref, bf16[768,1536]{1,0:T(8,128)(2,1)S(1)} %get-tuple-element.22.kv_ref, bf16[768,768]{1,0:T(8,128)(2,1)S(1)} %get-tuple-element.23.mix_ref, ...), custom_call_target="tpu_custom_call" | custom-call | flops 30000001024 | bytes 8388608 | tf_op jit(solution)/shard_map/second/pallas_call | solution.py:363
  21.7 27.7 %all_to_all.10 = bf16[128,3,2,768]{3,2,1,0:T(2,128)(2,1)S(1)} all-to-all(bf16[128,3,2,768]{3,2,1,0:T(2,128)(2,1)S(1)} %bitcast.6), channel_id=1, replica_groups=mesh['row'=8,'col'=16] {'row','col'}, dimensions={0} | all-to-all | bytes 2359296 | tf_op jit(solution)/shard_map/all_to_all | solution.py:405
  49.5 0.0 slice-done
  49.5 0.0 slice-done.3
  49.5 0.0 slice-done.1
  49.5 0.0 slice-done.2
  49.5 0.0 slice-done.4
  49.5 0.0 slice-done.5
  49.5 9.2 %experts.1 = bf16[384,2,768]{2,1,0:T(2,128)(2,1)S(1)} custom-call(bf16[384,2,768]{2,1,0:T(2,128)(2,1)S(1)} %bitcast.7, bf16[768,256]{1,0:T(8,128)(2,1)S(1)} %get-tuple-element.29.columns_ref, bf16[2,768,3072]{2,1,0:T(8,128)(2,1)S(1)} %bitcast.10, bf16[2,3072,768]{2,1,0:T(8,128)(2,1)S(1)} %bitcast.12), custom_call_target="tpu_custom_call" | custom-call | flops 7000000000 | bytes 20971520 | tf_op jit(solution)/shard_map/experts/pallas_call | solution.py:376
  58.8 24.5 %all_to_all.11 = bf16[128,3,2,768]{3,2,1,0:T(2,128)(2,1)S(1)} all-to-all(bf16[128,3,2,768]{3,2,1,0:T(2,128)(2,1)S(1)} %bitcast.8), channel_id=1, replica_groups=mesh['row'=8,'col'=16] {'row','col'}, dimensions={0} | all-to-all | bytes 2359296 | tf_op jit(solution)/shard_map/all_to_all | solution.py:405
  83.3 1.6 %last.1 = bf16[512,768]{1,0:T(8,128)(2,1)} custom-call(bf16[384,2,768]{2,1,0:T(2,128)(2,1)S(1)} %bitcast.5, bf16[256,768]{1,0:T(8,128)(2,1)S(1)} %get-tuple-element.30.hid0_ref, bf16[256,768]{1,0:T(8,128)(2,1)S(1)} %get-tuple-element.31.hid1_ref, s32[512,128]{1,0:T(8,128)S(1)} %get-tuple-element.32.wide_ref), custom_call_target="tpu_custom_call" | custom-call | flops 600000000 | bytes 3145728 | tf_op jit(solution)/shard_map/last/pallas_call | solution.py:391
  (2 shorter events, 0.0 us)
Async XLA Ops:
  1.4 17.0 %collective-permute-start = (bf16[256,768]{1,0:T(8,128)(2,1)S(1)}, bf16[256,768]{1,0:T(8,128)(2,1)S(1)}, u32[]{:S(2)}, u32[]{:S(2)}) collective-permute-start(bf16[256,768]{1,0:T(8,128)(2,1)S(1)} %get-tuple-element.19.normed_ref), channel_id=1, source_target_pairs={{0,1},{1,2},{2,3},{3,4},{4,5},{5,6},{6,7},{7,8},{8,9},{9,10},{10,1... | collective-permute-start | bytes 1179656 | tf_op jit(solution)/shard_map/ppermute | solution.py:410
  5.4 44.1 %slice-start = ((s8[9437184]{0:T(1024)(128)(4,1)}), s8[4194304]{0:T(1024)(128)(4,1)S(1)}, s32[]{:S(2)}) async-start(s8[9437184]{0:T(1024)(128)(4,1)} %bitcast.9), calls=%async_computation.2 | async-start | bytes 8388608
  5.4 44.1 %slice-start.3 = ((s8[9437184]{0:T(1024)(128)(4,1)}), s8[1048576]{0:T(1024)(128)(4,1)S(1)}, s32[]{:S(2)}) async-start(s8[9437184]{0:T(1024)(128)(4,1)} %bitcast.11), calls=%async_computation.5 | async-start | bytes 2097152
  18.4 31.0 %slice-start.1 = ((s8[9437184]{0:T(1024)(128)(4,1)}), s8[4194304]{0:T(1024)(128)(4,1)S(1)}, s32[]{:S(2)}) async-start(s8[9437184]{0:T(1024)(128)(4,1)} %bitcast.9), calls=%async_computation.3 | async-start | bytes 8388608
  18.4 31.0 %slice-start.2 = ((s8[9437184]{0:T(1024)(128)(4,1)}), s8[1048576]{0:T(1024)(128)(4,1)S(1)}, s32[]{:S(2)}) async-start(s8[9437184]{0:T(1024)(128)(4,1)} %bitcast.9), calls=%async_computation.4 | async-start | bytes 2097152
  18.4 31.0 %slice-start.4 = ((s8[9437184]{0:T(1024)(128)(4,1)}), s8[4194304]{0:T(1024)(128)(4,1)S(1)}, s32[]{:S(2)}) async-start(s8[9437184]{0:T(1024)(128)(4,1)} %bitcast.11), calls=%async_computation.6 | async-start | bytes 8388608
  18.4 31.1 %slice-start.5 = ((s8[9437184]{0:T(1024)(128)(4,1)}), s8[4194304]{0:T(1024)(128)(4,1)S(1)}, s32[]{:S(2)}) async-start(s8[9437184]{0:T(1024)(128)(4,1)} %bitcast.11), calls=%async_computation.7 | async-start | bytes 8388608

commit v5 on v4

--- a/solution.py
+++ b/solution.py
@@ -157,9 +157,9 @@
     high.start()
     low.start()
     high.wait()
-    low.wait()
     for r in range(0, LOOK, 32):
         normed_out[r : r + 32, :] = norm_rows(high_out[r : r + 32, :].astype(F32))
+    apart(low.wait)
 
 
 def first_kernel(
@@ -215,8 +215,8 @@
             v0 = payload(v_s[:LOOK, c], half, ones)
             v1 = payload(v_s[LOOK:, c], half, ones)
             low += dot(own_weights(dot_t(q0, k0), ahead), v0)
-            high += dot(behind_weights(dot_t(q1, k0), behind), v0)
-            high += dot(own_weights(dot_t(q1, k1), ahead), v1)
+            both = jnp.concatenate([behind_weights(dot_t(q1, k0), behind), own_weights(dot_t(q1, k1), ahead)], axis=1)
+            high += dot(both, jnp.concatenate([v0, v1], axis=0))
         acc_out[:, pair * 256 : pair * 256 + 256] = low
         ctx[:, c] = (high[:, :LANES] / high[:, LANES:]).astype(BF)
     apart(mix[0].wait)
@@ -239,9 +239,12 @@
     for pair in range(PAIRS):
         c = slice(pair * LANES, pair * LANES + LANES)
         low = acc_ref[:, pair * 256 : pair * 256 + 256]
+        part = []
         for half in range(2):
             q0 = q_ref[:, c] * half_lanes(half)
-            low += dot(behind_weights(dot_t(q0, k_s[:, c]), behind), payload(v_s[:, c] * ones, half, ones))
+            part.append(behind_weights(dot_t(q0, k_s[:, c]), behind))
+        both = jnp.concatenate([payload(v_s[:, c], 0, ones), payload(v_s[:, c], 1, ones)], axis=0)
+        low += dot(jnp.concatenate(part, axis=1), both)
         ctx[:, c] = (low[:, :LANES] / low[:, LANES:]).astype(BF)
     finish(ctx, mix_ref, x_ref, hid_out, routed)
     for s in range(0, SLOTS, 256):

time: 85.2 us -> 84.7 us (level)
  no operation moved by 1% of the time
where the time goes in v5:
time: 84.7 us; the launch traced here: 84.6 us
  blocking collectives  52.1 us (62%)
  Pallas kernels  25.1 us (30%)
  starting transfers between devices  3.95 us (5%)
  waiting for transfers between devices  3.16 us (4%)
    all_to_all x2, blocking collectives, exchange(): lax.all_to_all(rows, AXES, split_axis=0, concat_axis=0, tiled=True)  52.1 us
    pallas_call x1, Pallas kernels, call_first(): pl.pallas_call(first_kernel, out_shape=(shape(LOOK, D), shape(LOOK, 2 * D...  9.85 us
    pallas_call x1, Pallas kernels, call_experts(): pl.pallas_call(expert_kernel, out_shape=shape(SLOTS // 2, 2, D), scratch_...  9.24 us
    ppermute x1, starting transfers between devices, shards(): halo = lax.ppermute(normed, AXES, [(i, i + 1) for i in range(127)])  3.95 us
    ppermute x1, waiting for transfers between devices, shards(): halo = lax.ppermute(normed, AXES, [(i, i + 1) for i in range(127)])  3.16 us
    pallas_call x1, Pallas kernels, call_second(): pl.pallas_call(second_kernel, out_shape=(shape(SLOTS // 2, 2, D), shape(L...  3.11 us
  transfers between devices with their start and end apart: 1, of which 1 were waited for; matrix products, arithmetic and copies ran while one was open for 0% of the time, Pallas kernels for 12%

profile of v5, /device:TPU:1, one launch (start us, length us, event | category | flops | bytes accessed | tf_op | source)
XLA Modules:
  0.0 84.6 jit_solution(15008650723696773348)
XLA Ops:
  0.0 1.3 %load.1 = (bf16[256,768]{1,0:T(8,128)(2,1)S(1)}, bf16[256,768]{1,0:T(8,128)(2,1)S(1)}, bf16[256,768]{1,0:T(8,128)(2,1)S(1)}) custom-call(bf16[512,768]{1,0:T(8,128)(2,1)} %x_hbm.1), custom_call_target="tpu_custom_call" | custom-call | flops 1000000 | bytes 1048576 | tf_op jit(solution)/shard_map/load/pallas_call | solution.py:321
  1.3 3.9 %collective-permute-start = (bf16[256,768]{1,0:T(8,128)(2,1)S(1)}, bf16[256,768]{1,0:T(8,128)(2,1)S(1)}, u32[]{:S(2)}, u32[]{:S(2)}) collective-permute-start(bf16[256,768]{1,0:T(8,128)(2,1)S(1)} %get-tuple-element.19.normed_ref), channel_id=1, source_target_pairs={{0,1},{1,2},{2,3},{3,4},{4,5},{5,6},{6,7},{7,8},{8,9},{9,10},{10,1... | collective-permute-start | bytes 1179656 | tf_op jit(solution)/shard_map/ppermute | solution.py:413
  5.3 0.0 slice-start
  5.3 0.0 slice-start.3
  5.3 9.8 %first.1 = (bf16[256,768]{1,0:T(8,128)(2,1)S(1)}, f32[256,1536]{1,0:T(8,128)S(1)}, bf16[256,768]{1,0:T(8,128)(2,1)S(1)}, bf16[768,768]{1,0:T(8,128)(2,1)S(1)}, s...) custom-call(bf16[256,768]{1,0:T(8,128)(2,1)S(1)} %get-tuple-element., ...), custom_call_target="tpu_custom_call" | custom-call | flops 4000000000 | bytes 8388608 | tf_op jit(solution)/shard_map/first/pallas_call | solution.py:334
  15.2 3.2 %collective-permute-done.halo_ref = bf16[256,768]{1,0:T(8,128)(2,1)S(1)} collective-permute-done((bf16[256,768]{1,0:T(8,128)(2,1)S(1)}, bf16[256,768]{1,0:T(8,128)(2,1)S(1)}, u32[]{:S(2)}, u32[]{:S(2)}) %collective-permute-start) | collective-permute-done | bytes 393248 | tf_op jit(solution)/shard_map/ppermute | solution.py:413
  18.3 0.0 slice-start.1
  18.3 0.0 slice-start.2
  18.3 0.0 slice-start.4
  18.3 0.0 slice-start.5
  18.3 3.1 %second.1 = (bf16[384,2,768]{2,1,0:T(2,128)(2,1)S(1)}, bf16[256,768]{1,0:T(8,128)(2,1)S(1)}) custom-call(bf16[256,768]{1,0:T(8,128)(2,1)S(1)} %collective-permute-done.halo_ref, bf16[768,1536]{1,0:T(8,128)(2,1)S(1)} %get-tuple-element.22.kv_ref, bf16[768,768]{1,0:T(8,128)(2,1)S(1)} %get-tuple-element.23.mix_ref, ...), custom_call_target="tpu_custom_call" | custom-call | flops 30000001024 | bytes 8388608 | tf_op jit(solution)/shard_map/second/pallas_call | solution.py:366
  21.4 27.6 %all_to_all.10 = bf16[128,3,2,768]{3,2,1,0:T(2,128)(2,1)S(1)} all-to-all(bf16[128,3,2,768]{3,2,1,0:T(2,128)(2,1)S(1)} %bitcast.6), channel_id=1, replica_groups=mesh['row'=8,'col'=16] {'row','col'}, dimensions={0} | all-to-all | bytes 2359296 | tf_op jit(solution)/shard_map/all_to_all | solution.py:408
  49.0 0.0 slice-done
  49.0 0.0 slice-done.3
  49.0 0.0 slice-done.1
  49.0 0.0 slice-done.2
  49.0 0.0 slice-done.4
  49.0 0.0 slice-done.5
  49.1 9.2 %experts.1 = bf16[384,2,768]{2,1,0:T(2,128)(2,1)S(1)} custom-call(bf16[384,2,768]{2,1,0:T(2,128)(2,1)S(1)} %bitcast.7, bf16[768,256]{1,0:T(8,128)(2,1)S(1)} %get-tuple-element.29.columns_ref, bf16[2,768,3072]{2,1,0:T(8,128)(2,1)S(1)} %bitcast.10, bf16[2,3072,768]{2,1,0:T(8,128)(2,1)S(1)} %bitcast.12), custom_call_target="tpu_custom_call" | custom-call | flops 7000000000 | bytes 20971520 | tf_op jit(solution)/shard_map/experts/pallas_call | solution.py:379
  58.3 24.5 %all_to_all.11 = bf16[128,3,2,768]{3,2,1,0:T(2,128)(2,1)S(1)} all-to-all(bf16[128,3,2,768]{3,2,1,0:T(2,128)(2,1)S(1)} %bitcast.8), channel_id=1, replica_groups=mesh['row'=8,'col'=16] {'row','col'}, dimensions={0} | all-to-all | bytes 2359296 | tf_op jit(solution)/shard_map/all_to_all | solution.py:408
  82.8 1.6 %last.1 = bf16[512,768]{1,0:T(8,128)(2,1)} custom-call(bf16[384,2,768]{2,1,0:T(2,128)(2,1)S(1)} %bitcast.5, bf16[256,768]{1,0:T(8,128)(2,1)S(1)} %get-tuple-element.30.hid0_ref, bf16[256,768]{1,0:T(8,128)(2,1)S(1)} %get-tuple-element.31.hid1_ref, s32[512,128]{1,0:T(8,128)S(1)} %get-tuple-element.32.wide_ref), custom_call_target="tpu_custom_call" | custom-call | flops 600000000 | bytes 3145728 | tf_op jit(solution)/shard_map/last/pallas_call | solution.py:394
  (2 shorter events, 0.0 us)
Async XLA Ops:
  1.3 17.0 %collective-permute-start = (bf16[256,768]{1,0:T(8,128)(2,1)S(1)}, bf16[256,768]{1,0:T(8,128)(2,1)S(1)}, u32[]{:S(2)}, u32[]{:S(2)}) collective-permute-start(bf16[256,768]{1,0:T(8,128)(2,1)S(1)} %get-tuple-element.19.normed_ref), channel_id=1, source_target_pairs={{0,1},{1,2},{2,3},{3,4},{4,5},{5,6},{6,7},{7,8},{8,9},{9,10},{10,1... | collective-permute-start | bytes 1179656 | tf_op jit(solution)/shard_map/ppermute | solution.py:413
  5.3 43.7 %slice-start = ((s8[9437184]{0:T(1024)(128)(4,1)}), s8[4194304]{0:T(1024)(128)(4,1)S(1)}, s32[]{:S(2)}) async-start(s8[9437184]{0:T(1024)(128)(4,1)} %bitcast.9), calls=%async_computation.2 | async-start | bytes 8388608
  5.3 43.7 %slice-start.3 = ((s8[9437184]{0:T(1024)(128)(4,1)}), s8[1048576]{0:T(1024)(128)(4,1)S(1)}, s32[]{:S(2)}) async-start(s8[9437184]{0:T(1024)(128)(4,1)} %bitcast.11), calls=%async_computation.5 | async-start | bytes 2097152
  18.3 30.7 %slice-start.1 = ((s8[9437184]{0:T(1024)(128)(4,1)}), s8[4194304]{0:T(1024)(128)(4,1)S(1)}, s32[]{:S(2)}) async-start(s8[9437184]{0:T(1024)(128)(4,1)} %bitcast.9), calls=%async_computation.3 | async-start | bytes 8388608
  18.3 30.7 %slice-start.2 = ((s8[9437184]{0:T(1024)(128)(4,1)}), s8[1048576]{0:T(1024)(128)(4,1)S(1)}, s32[]{:S(2)}) async-start(s8[9437184]{0:T(1024)(128)(4,1)} %bitcast.9), calls=%async_computation.4 | async-start | bytes 2097152
  18.3 30.7 %slice-start.4 = ((s8[9437184]{0:T(1024)(128)(4,1)}), s8[4194304]{0:T(1024)(128)(4,1)S(1)}, s32[]{:S(2)}) async-start(s8[9437184]{0:T(1024)(128)(4,1)} %bitcast.11), calls=%async_computation.6 | async-start | bytes 8388608
  18.3 30.7 %slice-start.5 = ((s8[9437184]{0:T(1024)(128)(4,1)}), s8[4194304]{0:T(1024)(128)(4,1)S(1)}, s32[]{:S(2)}) async-start(s8[9437184]{0:T(1024)(128)(4,1)} %bitcast.11), calls=%async_computation.7 | async-start | bytes 8388608

commit v6 on v5

--- a/solution.py
+++ b/solution.py
@@ -151,23 +151,21 @@
     lax.fori_loop(0, jnp.minimum(device_index(), 0) + 1, step, 0)
 
 
-def load_kernel(x_hbm, low_out, high_out, normed_out, sems):
-    high = pltpu.make_async_copy(x_hbm.at[pl.ds(LOOK, LOOK), :], high_out, sems.at[0])
-    low = pltpu.make_async_copy(x_hbm.at[pl.ds(0, LOOK), :], low_out, sems.at[1])
+def load_kernel(x_hbm, high_out, normed_out, sem):
+    high = pltpu.make_async_copy(x_hbm.at[pl.ds(LOOK, LOOK), :], high_out, sem)
     high.start()
-    low.start()
     high.wait()
     for r in range(0, LOOK, 32):
         normed_out[r : r + 32, :] = norm_rows(high_out[r : r + 32, :].astype(F32))
-    apart(low.wait)
 
 
 def first_kernel(
-    low_ref, high_ref, normed_ref, scale_hbm, w_hbm, mix_hbm, columns_hbm, row_hbm,
-    q_out, acc_out, hid_out, buf_out, flat_out, wide_out, kv_out, mix_ref, columns_out,
+    high_ref, normed_ref, x_hbm, scale_hbm, w_hbm, mix_hbm, columns_hbm, row_hbm,
+    q_out, acc_out, hid_out, buf_out, flat_out, wide_out, low_ref, kv_out, mix_ref, columns_out,
     normed, wq, q_s, k_s, v_s, ctx, routed, columns_ref, row_ref, scale_ref, sems,
 ):
     early = [
+        pltpu.make_async_copy(x_hbm.at[pl.ds(0, LOOK), :], low_ref, sems.at[0]),
         pltpu.make_async_copy(row_hbm, row_ref, sems.at[5]),
         pltpu.make_async_copy(columns_hbm, columns_ref, sems.at[3]),
     ]
@@ -320,17 +318,17 @@
 def call_load(x):
     return pl.pallas_call(
         load_kernel,
-        out_shape=(shape(LOOK, D),) * 3,
+        out_shape=(shape(LOOK, D),) * 2,
         in_specs=[HB],
-        out_specs=(VM,) * 3,
-        scratch_shapes=[pltpu.SemaphoreType.DMA((2,))],
+        out_specs=(VM,) * 2,
+        scratch_shapes=[pltpu.SemaphoreType.DMA],
         compiler_params=params(8),
         cost_estimate=cost(10**6, MB),
         name="load",
     )(far(x))
 
 
-def call_first(low, high, normed, scaling, triple, mixing, columns, row):
+def call_first(high, normed, x, scaling, triple, mixing, columns, row):
     return pl.pallas_call(
         first_kernel,
         out_shape=(
@@ -340,12 +338,13 @@
             shape(SLOTS, D),
             shape(1, T, dtype=jnp.int32),
             shape(T, LANES, dtype=jnp.int32),
+            shape(LOOK, D),
             shape(D, 2 * D),
             shape(D, D),
             shape(D, 256),
         ),
-        in_specs=[VM] * 3 + [HB] * 5,
-        out_specs=(VM,) * 9,
+        in_specs=[VM] * 2 + [HB] * 6,
+        out_specs=(VM,) * 10,
         scratch_shapes=[pltpu.VMEM((T, D), BF), pltpu.VMEM((D, D), BF)]
         + [pltpu.VMEM((T, D), BF)] * 3
         + [
@@ -359,7 +358,7 @@
         compiler_params=params(16),
         cost_estimate=cost(4 * 10**9, 8 * MB),
         name="first",
-    )(low, high, normed, *(far(a) for a in (scaling, triple, mixing, columns, row)))
+    )(high, normed, *(far(a) for a in (x, scaling, triple, mixing, columns, row)))
 
 
 def call_second(halo, kv, mixing, x, q0, acc0, buf1, flat):
@@ -409,10 +408,10 @@
 
 
 def shards(x, triple, mixing, scaling, columns, pick, entry, exits):
-    low, high, normed = call_load(x)
+    high, normed = call_load(x)
     halo = lax.ppermute(normed, AXES, [(i, i + 1) for i in range(127)])
-    first = call_first(low, high, normed, scaling, triple, mixing, columns, pick.reshape(1, T))
-    q0, acc0, hid1, buf1, flat, wide, kv, mix_near, columns_near = first
+    first = call_first(high, normed, x, scaling, triple, mixing, columns, pick.reshape(1, T))
+    q0, acc0, hid1, buf1, flat, wide, low, kv, mix_near, columns_near = first
     buf, hid0 = call_second(halo, kv, mix_near, low, q0, acc0, buf1, flat)
     back = exchange(call_experts(exchange(buf), columns_near, entry, exits))
     return call_last(back, hid0, hid1, wide)

time: 84.7 us -> 84.9 us (level)
  no operation moved by 1% of the time
where the time goes in v6:
time: 84.9 us; the launch traced here: 84.7 us
  blocking collectives  52.2 us (61%)
  Pallas kernels  25.2 us (30%)
  starting transfers between devices  3.95 us (5%)
  waiting for transfers between devices  3.04 us (4%)
    all_to_all x2, blocking collectives, exchange(): lax.all_to_all(rows, AXES, split_axis=0, concat_axis=0, tiled=True)  52.2 us
    pallas_call x1, Pallas kernels, call_first(): pl.pallas_call(first_kernel, out_shape=(shape(LOOK, D), shape(LOOK, 2 * D...  9.98 us
    pallas_call x1, Pallas kernels, call_experts(): pl.pallas_call(expert_kernel, out_shape=shape(SLOTS // 2, 2, D), scratch_...  9.24 us
    ppermute x1, starting transfers between devices, shards(): halo = lax.ppermute(normed, AXES, [(i, i + 1) for i in range(127)])  3.95 us
    pallas_call x1, Pallas kernels, call_second(): pl.pallas_call(second_kernel, out_shape=(shape(SLOTS // 2, 2, D), shape(L...  3.13 us
    ppermute x1, waiting for transfers between devices, shards(): halo = lax.ppermute(normed, AXES, [(i, i + 1) for i in range(127)])  3.04 us
  transfers between devices with their start and end apart: 1, of which 1 were waited for; matrix products, arithmetic and copies ran while one was open for 0% of the time, Pallas kernels for 12%

profile of v6, /device:TPU:1, one launch (start us, length us, event | category | flops | bytes accessed | tf_op | source)
XLA Modules:
  0.0 84.7 jit_solution(12032127611138393685)
XLA Ops:
  0.0 1.3 %load.1 = (bf16[256,768]{1,0:T(8,128)(2,1)S(1)}, bf16[256,768]{1,0:T(8,128)(2,1)S(1)}) custom-call(bf16[512,768]{1,0:T(8,128)(2,1)} %x_hbm.3), custom_call_target="tpu_custom_call" | custom-call | flops 1000000 | bytes 1048576 | tf_op jit(solution)/shard_map/load/pallas_call | solution.py:319
  1.3 3.9 %collective-permute-start = (bf16[256,768]{1,0:T(8,128)(2,1)S(1)}, bf16[256,768]{1,0:T(8,128)(2,1)S(1)}, u32[]{:S(2)}, u32[]{:S(2)}) collective-permute-start(bf16[256,768]{1,0:T(8,128)(2,1)S(1)} %get-tuple-element.19.normed_ref), channel_id=1, source_target_pairs={{0,1},{1,2},{2,3},{3,4},{4,5},{5,6},{6,7},{7,8},{8,9},{9,10},{10,1... | collective-permute-start | bytes 1179656 | tf_op jit(solution)/shard_map/ppermute | solution.py:412
  5.3 0.0 slice-start
  5.3 0.0 slice-start.3
  5.3 10.0 %first.1 = (bf16[256,768]{1,0:T(8,128)(2,1)S(1)}, f32[256,1536]{1,0:T(8,128)S(1)}, bf16[256,768]{1,0:T(8,128)(2,1)S(1)}, bf16[768,768]{1,0:T(8,128)(2,1)S(1)}, s...) custom-call(bf16[256,768]{1,0:T(8,128)(2,1)S(1)} %get-tuple-element., ...), custom_call_target="tpu_custom_call" | custom-call | flops 4000000000 | bytes 8388608 | tf_op jit(solution)/shard_map/first/pallas_call | solution.py:332
  15.3 3.0 %collective-permute-done.halo_ref = bf16[256,768]{1,0:T(8,128)(2,1)S(1)} collective-permute-done((bf16[256,768]{1,0:T(8,128)(2,1)S(1)}, bf16[256,768]{1,0:T(8,128)(2,1)S(1)}, u32[]{:S(2)}, u32[]{:S(2)}) %collective-permute-start) | collective-permute-done | bytes 393248 | tf_op jit(solution)/shard_map/ppermute | solution.py:412
  18.3 0.0 slice-start.1
  18.3 0.0 slice-start.2
  18.3 0.0 slice-start.4
  18.3 0.0 slice-start.5
  18.3 3.1 %second.1 = (bf16[384,2,768]{2,1,0:T(2,128)(2,1)S(1)}, bf16[256,768]{1,0:T(8,128)(2,1)S(1)}) custom-call(bf16[256,768]{1,0:T(8,128)(2,1)S(1)} %collective-permute-done.halo_ref, bf16[768,1536]{1,0:T(8,128)(2,1)S(1)} %get-tuple-element.21.kv_ref, bf16[768,768]{1,0:T(8,128)(2,1)S(1)} %get-tuple-element.22.mix_ref, ...), custom_call_target="tpu_custom_call" | custom-call | flops 30000001024 | bytes 8388608 | tf_op jit(solution)/shard_map/second/pallas_call | solution.py:365
  21.4 27.7 %all_to_all.10 = bf16[128,3,2,768]{3,2,1,0:T(2,128)(2,1)S(1)} all-to-all(bf16[128,3,2,768]{3,2,1,0:T(2,128)(2,1)S(1)} %bitcast.6), channel_id=1, replica_groups=mesh['row'=8,'col'=16] {'row','col'}, dimensions={0} | all-to-all | bytes 2359296 | tf_op jit(solution)/shard_map/all_to_all | solution.py:407
  49.1 0.0 slice-done
  49.1 0.0 slice-done.3
  49.1 0.0 slice-done.1
  49.1 0.0 slice-done.2
  49.1 0.0 slice-done.4
  49.2 0.0 slice-done.5
  49.2 9.2 %experts.1 = bf16[384,2,768]{2,1,0:T(2,128)(2,1)S(1)} custom-call(bf16[384,2,768]{2,1,0:T(2,128)(2,1)S(1)} %bitcast.7, bf16[768,256]{1,0:T(8,128)(2,1)S(1)} %get-tuple-element.29.columns_ref, bf16[2,768,3072]{2,1,0:T(8,128)(2,1)S(1)} %bitcast.10, bf16[2,3072,768]{2,1,0:T(8,128)(2,1)S(1)} %bitcast.12), custom_call_target="tpu_custom_call" | custom-call | flops 7000000000 | bytes 20971520 | tf_op jit(solution)/shard_map/experts/pallas_call | solution.py:378
  58.4 24.5 %all_to_all.11 = bf16[128,3,2,768]{3,2,1,0:T(2,128)(2,1)S(1)} all-to-all(bf16[128,3,2,768]{3,2,1,0:T(2,128)(2,1)S(1)} %bitcast.8), channel_id=1, replica_groups=mesh['row'=8,'col'=16] {'row','col'}, dimensions={0} | all-to-all | bytes 2359296 | tf_op jit(solution)/shard_map/all_to_all | solution.py:407
  83.0 1.6 %last.1 = bf16[512,768]{1,0:T(8,128)(2,1)} custom-call(bf16[384,2,768]{2,1,0:T(2,128)(2,1)S(1)} %bitcast.5, bf16[256,768]{1,0:T(8,128)(2,1)S(1)} %get-tuple-element.30.hid0_ref, bf16[256,768]{1,0:T(8,128)(2,1)S(1)} %get-tuple-element.31.hid1_ref, s32[512,128]{1,0:T(8,128)S(1)} %get-tuple-element.32.wide_ref), custom_call_target="tpu_custom_call" | custom-call | flops 600000000 | bytes 3145728 | tf_op jit(solution)/shard_map/last/pallas_call | solution.py:393
  (2 shorter events, 0.0 us)
Async XLA Ops:
  1.3 17.0 %collective-permute-start = (bf16[256,768]{1,0:T(8,128)(2,1)S(1)}, bf16[256,768]{1,0:T(8,128)(2,1)S(1)}, u32[]{:S(2)}, u32[]{:S(2)}) collective-permute-start(bf16[256,768]{1,0:T(8,128)(2,1)S(1)} %get-tuple-element.19.normed_ref), channel_id=1, source_target_pairs={{0,1},{1,2},{2,3},{3,4},{4,5},{5,6},{6,7},{7,8},{8,9},{9,10},{10,1... | collective-permute-start | bytes 1179656 | tf_op jit(solution)/shard_map/ppermute | solution.py:412
  5.3 43.9 %slice-start = ((s8[9437184]{0:T(1024)(128)(4,1)}), s8[4194304]{0:T(1024)(128)(4,1)S(1)}, s32[]{:S(2)}) async-start(s8[9437184]{0:T(1024)(128)(4,1)} %bitcast.9), calls=%async_computation.2 | async-start | bytes 8388608
  5.3 43.9 %slice-start.3 = ((s8[9437184]{0:T(1024)(128)(4,1)}), s8[1048576]{0:T(1024)(128)(4,1)S(1)}, s32[]{:S(2)}) async-start(s8[9437184]{0:T(1024)(128)(4,1)} %bitcast.11), calls=%async_computation.5 | async-start | bytes 2097152
  18.3 30.8 %slice-start.1 = ((s8[9437184]{0:T(1024)(128)(4,1)}), s8[4194304]{0:T(1024)(128)(4,1)S(1)}, s32[]{:S(2)}) async-start(s8[9437184]{0:T(1024)(128)(4,1)} %bitcast.9), calls=%async_computation.3 | async-start | bytes 8388608
  18.3 30.8 %slice-start.2 = ((s8[9437184]{0:T(1024)(128)(4,1)}), s8[1048576]{0:T(1024)(128)(4,1)S(1)}, s32[]{:S(2)}) async-start(s8[9437184]{0:T(1024)(128)(4,1)} %bitcast.9), calls=%async_computation.4 | async-start | bytes 2097152
  18.3 30.8 %slice-start.4 = ((s8[9437184]{0:T(1024)(128)(4,1)}), s8[4194304]{0:T(1024)(128)(4,1)S(1)}, s32[]{:S(2)}) async-start(s8[9437184]{0:T(1024)(128)(4,1)} %bitcast.11), calls=%async_computation.6 | async-start | bytes 8388608
  18.3 30.8 %slice-start.5 = ((s8[9437184]{0:T(1024)(128)(4,1)}), s8[4194304]{0:T(1024)(128)(4,1)S(1)}, s32[]{:S(2)}) async-start(s8[9437184]{0:T(1024)(128)(4,1)} %bitcast.11), calls=%async_computation.7 | async-start | bytes 8388608
